TPU v7x, 32 devices: a whole 2x2x4 slice. The times are simulated.
32 devices in a mesh: group: 4 (over y, core), mp: 8 (over z, x).
Axes of the slice: x: 2, y: 2, z: 4, core: 2. Of those that a mesh axis runs over, the one named last changes fastest.
Arguments:
- layer_in: float32 [256, 64, 768], P(('group', 'mp')), may hold values from -8 to 8
- cotangent: float32 [256, 64, 768], P(('group', 'mp')), may hold values from -6 to 6
- target: int32 [256], P(('group', 'mp')), may hold values from 0 to 3
- keep_mask: int32 [256], P(('group', 'mp')), may hold values from 0 to 1
- capacity: int32 [4], replicated, may hold values from 1 to 2, as said below
- attention_weights: float32 [4, 4, 768, 768], P('group', None, 'mp')
- feedforward_weights: float32 [4, 2, 768, 3072], P('group', None, 'mp')
- vectors: float32 [4, 12, 768], P('group', None, 'mp')
- row_moments: float32 [4, 6, 768], P('group', None, 'mp'), as said below
- column_moments: float32 [4, 9216], P('group'), as said below
- vector_moments: float32 [4, 12, 768], P('group', None, 'mp'), as said below
Outputs:
- layer_out: float32 [256, 64, 768], P(('group', 'mp'))
- input_grad: float32 [256, 64, 768], P(('group', 'mp'))
- attention_grad: float32 [4, 4, 768, 768], P('group', None, 'mp')
- feedforward_grad: float32 [4, 2, 768, 3072], P('group', None, 'mp')
- vectors_grad: float32 [4, 12, 768], P('group', None, 'mp')
- renewed_rows: float32 [4, 6, 768], P('group', None, 'mp')
- renewed_columns: float32 [4, 9216], P('group')
- renewed_vectors: float32 [4, 12, 768], P('group', None, 'mp')
- attention_updated: float32 [4, 4, 768, 768], P('group', None, 'mp')
- feedforward_updated: float32 [4, 2, 768, 3072], P('group', None, 'mp')
- vectors_updated: float32 [4, 12, 768], P('group', None, 'mp')
- update_scale: float32 [4, 18], P('group')
Inputs may be any that keep to these rules, and one draw needn't show every extreme that they name: Some group has capacity 2, and every block of 8 sequences holds 2 or more sequences with keep_mask 1 whose target is a group of capacity 2. `row_moments`: positive. `column_moments`: positive. `vector_moments`: positive.
All inputs are finite; a program needn't handle non-finite values.
Results may differ from a plain program's by a relative error of at most 0.012.
The roundings to bfloat16 on the way count: a program that leaves them out, or rounds other values in their place, can miss the bound.
Values may be sent and summed in bfloat16 or wider, within the bound.
A program may use at most 192 MiB of HBM per device.

v0:
```python
import jax
import jax.numpy as jnp
from jax import lax
from jax.sharding import PartitionSpec as P

HEADS = 12
SLOTS = 2
STEP = 10


epsilon = 1e-05
tiny_square = 1e-30
clip_level = 1.0
matrix_rate = 0.01
vector_rate = 0.1


def normalize(stream, gains, shifts):
    center = stream - jnp.mean(stream, axis=-1, keepdims=True)
    inverse = lax.rsqrt(jnp.mean(center * center, axis=-1, keepdims=True) + epsilon)
    normed = center * inverse
    return (normed * gains + shifts, normed, inverse)


def normalize_back(upstream, gains, normed, inverse):
    scaled = upstream * gains
    return inverse * (
        scaled
        - jnp.mean(scaled, axis=-1, keepdims=True)
        - normed * jnp.mean(scaled * normed, axis=-1, keepdims=True)
    )


def gelu_exact(tensor):
    return jax.nn.gelu(tensor, approximate=False)


def body(
    layer_in,
    cotangent,
    target,
    keep_mask,
    capacity,
    attention_weights,
    feedforward_weights,
    vectors,
    row_moments,
    column_moments,
    vector_moments,
):
    group_count = lax.axis_size("group")
    local_count = layer_in.shape[0]
    seq_len = layer_in.shape[1]
    model_width = layer_in.shape[2]
    head_dim = model_width // HEADS
    hidden = feedforward_weights.shape[3]
    slot_count = SLOTS
    buffered = group_count * slot_count
    row_total = buffered * seq_len
    score_scale = head_dim ** (-0.5)
    group_ids = jnp.arange(group_count, dtype=jnp.int32)
    aimed_at = (target[:, None] == group_ids[None, :]).astype(jnp.int32)
    wanted = aimed_at * keep_mask[:, None]
    earlier = jnp.cumsum(wanted, axis=0) - wanted
    position = jnp.sum(earlier * aimed_at, axis=1)
    allowed = jnp.sum(aimed_at * capacity[None, :], axis=1)
    admitted = (keep_mask == 1) & (position < allowed)
    placed = target * slot_count + position
    cell_ids = jnp.arange(buffered, dtype=jnp.int32)
    matched = admitted[:, None] & (placed[:, None] == cell_ids[None, :])
    local_ids = jnp.arange(local_count, dtype=jnp.int32)
    source = jnp.sum(jnp.where(matched, local_ids[:, None], 0), axis=0) + jnp.where(
        jnp.any(matched, axis=0), 0, local_count
    )
    blank_row = jnp.zeros((1, seq_len, model_width), jnp.float32)
    send_inputs = jnp.take(jnp.concatenate([layer_in, blank_row], axis=0), source, axis=0).reshape(
        group_count, slot_count, seq_len, model_width
    )
    send_grads = jnp.take(jnp.concatenate([cotangent, blank_row], axis=0), source, axis=0).reshape(
        group_count, slot_count, seq_len, model_width
    )
    got_inputs, got_grads = (
        lax.all_to_all(send_inputs, "group", split_axis=0, concat_axis=0, tiled=True),
        lax.all_to_all(send_grads, "group", split_axis=0, concat_axis=0, tiled=True),
    )
    attention_full, feedforward_full, vectors_full = (
        lax.all_gather(attention_weights[0].astype(jnp.bfloat16), "mp", axis=1, tiled=True),
        lax.all_gather(feedforward_weights[0].astype(jnp.bfloat16), "mp", axis=1, tiled=True),
        lax.all_gather(vectors[0].astype(jnp.bfloat16), "mp", axis=1, tiled=True),
    )
    vector_rows = vectors_full.astype(jnp.float32)
    bias_query = vector_rows[0]
    bias_value = vector_rows[1]
    bias_output = vector_rows[2]
    gain_first = vector_rows[3]
    shift_first = vector_rows[4]
    bias_down = vector_rows[5]
    gain_second = vector_rows[6]
    shift_second = vector_rows[7]
    bias_up = vector_rows[8:12].reshape(-1)
    inputs = got_inputs.reshape(row_total, model_width)
    inputs_low = inputs.astype(jnp.bfloat16)
    projected = jnp.einsum(
        "rd,cde->cre", inputs_low, attention_full[:3], preferred_element_type=jnp.float32
    )
    projection_bias = jnp.stack([bias_query, jnp.zeros_like(bias_query), bias_value])
    projected_low = (projected + projection_bias[:, None, :]).astype(jnp.bfloat16)
    queries = projected_low[0].reshape(buffered, seq_len, HEADS, head_dim)
    key_rows = projected_low[1].reshape(buffered, seq_len, HEADS, head_dim)
    values = projected_low[2].reshape(buffered, seq_len, HEADS, head_dim)
    scores = (
        jnp.einsum("nshe,nthe->nhst", queries, key_rows, preferred_element_type=jnp.float32)
        * score_scale
    )
    largest = jnp.max(scores, axis=-1, keepdims=True)
    shifted = jnp.exp(scores - largest)
    totals = jnp.sum(shifted, axis=-1, keepdims=True)
    log_totals = largest + jnp.log(totals)
    weights_low = (shifted / totals).astype(jnp.bfloat16)
    attended = jnp.einsum(
        "nhst,nthe->nshe", weights_low, values, preferred_element_type=jnp.float32
    )
    attended_low = attended.reshape(row_total, model_width).astype(jnp.bfloat16)
    branch = (
        jnp.dot(attended_low, attention_full[3], preferred_element_type=jnp.float32) + bias_output
    )
    first_norm, normed_first, inverse_first = normalize(inputs + branch, gain_first, shift_first)
    first_low = first_norm.astype(jnp.bfloat16)
    before_act = (
        jnp.dot(first_low, feedforward_full[0], preferred_element_type=jnp.float32) + bias_up
    )
    activated = gelu_exact(before_act).astype(jnp.bfloat16)
    down_branch = (
        jnp.einsum("rf,df->rd", activated, feedforward_full[1], preferred_element_type=jnp.float32)
        + bias_down
    )
    output_rows, normed_second, inverse_second = normalize(
        first_norm + down_branch, gain_second, shift_second
    )
    returned = lax.all_to_all(
        output_rows.reshape(group_count, slot_count, seq_len, model_width),
        "group",
        split_axis=0,
        concat_axis=0,
        tiled=True,
    )
    upstream = got_grads.reshape(row_total, model_width)
    grad_gain_second = jnp.sum(upstream * normed_second, axis=0)
    grad_shift_second = jnp.sum(upstream, axis=0)
    grad_second = normalize_back(upstream, gain_second, normed_second, inverse_second)
    grad_down = grad_second.astype(jnp.bfloat16)
    grad_bias_down = jnp.sum(grad_down.astype(jnp.float32), axis=0)
    grad_w_down = jnp.einsum("rd,rf->df", grad_down, activated, preferred_element_type=jnp.float32)
    grad_activated = jnp.dot(grad_down, feedforward_full[1], preferred_element_type=jnp.float32)
    gelu_pull = jax.vjp(gelu_exact, before_act)[1]
    grad_before = gelu_pull(grad_activated)[0].astype(jnp.bfloat16)
    grad_bias_up = jnp.sum(grad_before.astype(jnp.float32), axis=0)
    grad_w_up = jnp.einsum("rd,rf->df", first_low, grad_before, preferred_element_type=jnp.float32)
    grad_first = grad_second + jnp.einsum(
        "rf,df->rd", grad_before, feedforward_full[0], preferred_element_type=jnp.float32
    )
    feedforward_grads = jnp.stack([grad_w_up, grad_w_down])
    grad_gain_first = jnp.sum(grad_first * normed_first, axis=0)
    grad_shift_first = jnp.sum(grad_first, axis=0)
    grad_residual = normalize_back(grad_first, gain_first, normed_first, inverse_first)
    grad_branch = grad_residual.astype(jnp.bfloat16)
    grad_bias_output = jnp.sum(grad_branch.astype(jnp.float32), axis=0)
    grad_w_output = jnp.einsum(
        "rd,re->de", attended_low, grad_branch, preferred_element_type=jnp.float32
    )
    grad_attended = jnp.einsum(
        "re,de->rd", grad_branch, attention_full[3], preferred_element_type=jnp.float32
    )
    grad_heads = grad_attended.astype(jnp.bfloat16).reshape(buffered, seq_len, HEADS, head_dim)
    again = (
        jnp.einsum("nshe,nthe->nhst", queries, key_rows, preferred_element_type=jnp.float32)
        * score_scale
    )
    exact = jnp.exp(again - log_totals)
    grad_values = jnp.einsum(
        "nhst,nshe->nthe",
        exact.astype(jnp.bfloat16),
        grad_heads,
        preferred_element_type=jnp.float32,
    ).astype(jnp.bfloat16)
    grad_weights = jnp.einsum(
        "nshe,nthe->nhst", grad_heads, values, preferred_element_type=jnp.float32
    )
    grad_scores = (
        exact * (grad_weights - jnp.sum(grad_weights * exact, axis=-1, keepdims=True))
    ).astype(jnp.bfloat16)
    grad_queries = (
        jnp.einsum("nhst,nthe->nshe", grad_scores, key_rows, preferred_element_type=jnp.float32)
        * score_scale
    ).astype(jnp.bfloat16)
    grad_keys = (
        jnp.einsum("nhst,nshe->nthe", grad_scores, queries, preferred_element_type=jnp.float32)
        * score_scale
    ).astype(jnp.bfloat16)
    grad_projected = jnp.stack(
        [
            grad_queries.reshape(row_total, model_width),
            grad_keys.reshape(row_total, model_width),
            grad_values.reshape(row_total, model_width),
        ]
    )
    grad_w_projected = jnp.einsum(
        "rd,cre->cde", inputs_low, grad_projected, preferred_element_type=jnp.float32
    )
    grad_inputs = grad_residual + jnp.einsum(
        "cre,cde->rd", grad_projected, attention_full[:3], preferred_element_type=jnp.float32
    )
    grad_bias_projected = jnp.sum(grad_projected.astype(jnp.float32), axis=1)
    grads_back = lax.all_to_all(
        grad_inputs.reshape(group_count, slot_count, seq_len, model_width),
        "group",
        split_axis=0,
        concat_axis=0,
        tiled=True,
    )
    attention_grads = jnp.concatenate([grad_w_projected, grad_w_output[None]], axis=0)
    vector_grads = jnp.concatenate(
        [
            jnp.stack(
                [
                    grad_bias_projected[0],
                    grad_bias_projected[2],
                    grad_bias_output,
                    grad_gain_first,
                    grad_shift_first,
                    grad_bias_down,
                    grad_gain_second,
                    grad_shift_second,
                ]
            ),
            grad_bias_up.reshape(4, model_width),
        ],
        axis=0,
    )
    attention_part, feedforward_part, vectors_part = (
        lax.psum_scatter(attention_grads, "mp", scatter_dimension=1, tiled=True),
        lax.psum_scatter(feedforward_grads, "mp", scatter_dimension=1, tiled=True),
        lax.psum_scatter(vector_grads, "mp", scatter_dimension=1, tiled=True),
    )
    slot_index = jnp.where(admitted, placed, 0)
    layer_out = jnp.where(
        admitted[:, None, None],
        jnp.take(returned.reshape(buffered, seq_len, model_width), slot_index, axis=0),
        layer_in,
    )
    input_grad = jnp.where(
        admitted[:, None, None],
        jnp.take(grads_back.reshape(buffered, seq_len, model_width), slot_index, axis=0),
        cotangent,
    )
    decay_rate = 1.0 - STEP ** (-0.8)
    keep_rate = 1.0 - decay_rate
    square_attention = attention_part * attention_part + tiny_square
    square_feedforward = feedforward_part * feedforward_part + tiny_square
    square_vectors = vectors_part * vectors_part + tiny_square
    rows_attention = decay_rate * row_moments[0, :4] + keep_rate * jnp.mean(
        square_attention, axis=-1
    )
    rows_feedforward = decay_rate * row_moments[0, 4:] + keep_rate * jnp.mean(
        square_feedforward, axis=-1
    )
    renewed_vectors = decay_rate * vector_moments[0] + keep_rate * square_vectors
    step_vectors = vectors_part / jnp.sqrt(renewed_vectors)
    vector_squares = jnp.sum(step_vectors * step_vectors, axis=-1)
    attention_columns = jnp.sum(square_attention, axis=1)
    feedforward_columns = jnp.sum(square_feedforward, axis=1)
    row_sums = jnp.concatenate(
        [jnp.sum(rows_attention, axis=-1), jnp.sum(rows_feedforward, axis=-1)]
    )
    old_attention = column_moments[0, : 4 * model_width].reshape(4, model_width)
    old_feedforward = column_moments[0, 4 * model_width :].reshape(2, hidden)
    attention_sums, feedforward_sums, rows_summed, vector_total = lax.psum(
        (attention_columns, feedforward_columns, row_sums, vector_squares), "mp"
    )
    columns_attention = decay_rate * old_attention + keep_rate * attention_sums / model_width
    columns_feedforward = decay_rate * old_feedforward + keep_rate * feedforward_sums / model_width
    mean_rows = rows_summed / model_width
    step_attention = attention_part / jnp.sqrt(
        rows_attention[:, :, None] * columns_attention[:, None, :] / mean_rows[:4, None, None]
    )
    step_feedforward = feedforward_part / jnp.sqrt(
        rows_feedforward[:, :, None] * columns_feedforward[:, None, :] / mean_rows[4:, None, None]
    )
    attention_total, feedforward_total = lax.psum(
        (
            jnp.sum(step_attention * step_attention, axis=(1, 2)),
            jnp.sum(step_feedforward * step_feedforward, axis=(1, 2)),
        ),
        "mp",
    )
    scale_attention = jnp.sqrt(attention_total / (model_width * model_width))
    scale_feedforward = jnp.sqrt(feedforward_total / (model_width * hidden))
    scale_vectors = jnp.sqrt(vector_total / model_width)
    attention_updated = (
        attention_weights[0]
        - matrix_rate
        * step_attention
        / jnp.maximum(1.0, scale_attention / clip_level)[:, None, None]
    )
    feedforward_updated = (
        feedforward_weights[0]
        - matrix_rate
        * step_feedforward
        / jnp.maximum(1.0, scale_feedforward / clip_level)[:, None, None]
    )
    vectors_updated = (
        vectors[0]
        - vector_rate * step_vectors / jnp.maximum(1.0, scale_vectors / clip_level)[:, None]
    )
    renewed_rows = jnp.concatenate([rows_attention, rows_feedforward], axis=0)
    renewed_columns = jnp.concatenate(
        [columns_attention.reshape(-1), columns_feedforward.reshape(-1)]
    )
    update_scale = jnp.concatenate([scale_attention, scale_feedforward, scale_vectors])
    return (
        layer_out,
        input_grad,
        attention_part[None],
        feedforward_part[None],
        vectors_part[None],
        renewed_rows[None],
        renewed_columns[None],
        renewed_vectors[None],
        attention_updated[None],
        feedforward_updated[None],
        vectors_updated[None],
        update_scale[None],
    )


def solution(mesh):
    in_specs = (
        P(("group", "mp"), None, None),
        P(("group", "mp"), None, None),
        P(("group", "mp")),
        P(("group", "mp")),
        P(),
        P("group", None, "mp", None),
        P("group", None, "mp", None),
        P("group", None, "mp"),
        P("group", None, "mp"),
        P("group", None),
        P("group", None, "mp"),
    )
    out_specs = (
        P(("group", "mp"), None, None),
        P(("group", "mp"), None, None),
        P("group", None, "mp", None),
        P("group", None, "mp", None),
        P("group", None, "mp"),
        P("group", None, "mp"),
        P("group", None),
        P("group", None, "mp"),
        P("group", None, "mp", None),
        P("group", None, "mp", None),
        P("group", None, "mp"),
        P("group", None),
    )
    return jax.shard_map(body, mesh=mesh, in_specs=in_specs, out_specs=out_specs, check_vma=False)
```

profile of v0, /device:TPU:0, one launch (start us, length us, event | category | flops | bytes accessed | tf_op | source)
XLA Modules:
  0.0 947.0 jit_solution(17386836779310034956)
XLA Ops:
  7.2 2.3 bitcast_convert_fusion.2
  19.5 3.0 broadcast_select_fusion
  22.5 24.1 %all_to_all.20 = f32[4,2,64,768]{3,2,1,0:T(8,128)S(1)} all-to-all(f32[4,2,64,768]{3,2,1,0:T(8,128)S(1)} %bitcast.160), channel_id=1, replica_groups=mesh['group'=4,'mp'=8] {'group'}, dimensions={0} | all-to-all | bytes 3145728 | tf_op jit(solution)/shard_map/all_to_all | solution.py:84
  46.7 3.8 all-to-all-start
  50.6 31.1 %all-gather = bf16[8,96,12]{1,2,0:T(8,128)(2,1)S(1)} all-gather(bf16[1,96,12]{1,2,0:T(8,128)(2,1)S(1)} %bitcast.170), channel_id=1, replica_groups=mesh['group'=4,'mp'=8] {'mp'}, dimensions={0}, use_global_device_ids=true | all-gather | bytes 20736 | tf_op jit(solution)/shard_map/all_gather | solution.py:89
  82.5 11.5 %all-gather.4.cloned.1.call-done = bf16[4,768,768]{2,1,0:T(8,128)(2,1)} async-done(((bf16[4,96,768]{2,1,0:T(8,128)(2,1)}), bf16[4,768,768]{2,1,0:T(8,128)(2,1)}) %all-gather.4.cloned.1.call-update) | async-done | bytes 4718608 | tf_op jit(solution)/shard_map/all_gather | solution.py:87
  94.0 4.0 fusion.15
  99.3 2.2 reshape.256
  102.8 2.9 copy.153
  107.0 2.9 copy.157
  109.9 2.7 multiply_reduce_fusion.1
  115.2 2.4 copy.149
  117.6 3.5 convert_element_type.99
  121.1 3.0 fusion.64
  125.5 107.6 %all-gather.6.cloned.1.call-done = bf16[2,768,3072]{2,1,0:T(8,128)(2,1)} async-done(((bf16[2,96,3072]{2,1,0:T(8,128)(2,1)}), bf16[2,768,3072]{2,1,0:T(8,128)(2,1)}) %all-gather.6.cloned.1.call-update) | async-done | bytes 9437200 | tf_op jit(solution)/shard_map/all_gather | solution.py:88
  233.1 20.2 %multiply_convert_fusion = (bf16[512,3072]{1,0:T(8,128)(2,1)S(1)}, f32[512,3072]{1,0:T(8,128)S(1)}, f32[512,3072]{1,0:T(8,128)}) fusion(f32[3072]{0:T(1024)S(1)} %add.182, bf16[2,768,3072]{2,1,0:T(8,128)(2,1)} %all-gather.6.cloned.1.call-done, f32[512,768]{1,0:T(8,128)} %copy-done.14, f32[768]{0:T(1024)S(1)} %get-tuple-element.65, ...), kind=kOutput, calls=%fused_computation.10 | convolution fusion | flops 2521694208 | bytes 22042624 | tf_op jit(solution)/shard_map/dot_general | solution.py:130
  253.3 2.8 fusion.65
  260.0 7.4 convert_reduce_fusion
  267.4 3.1 multiply_reduce_fusion.3
  272.2 3.0 convolution_convert_fusion.2
  275.2 3.8 reshape.259
  279.0 4.3 copy.161
  283.2 3.3 multiply_reduce_fusion
  293.8 2.2 convolution_bitcast_fusion.3
  298.3 2.5 copy.184
  302.9 3.5 copy.185
  306.4 2.2 reshape.241
  311.1 5.0 convolution_bitcast_fusion.2
  317.3 8.1 pad_maximum_fusion.1
  325.4 5.2 convolution_bitcast_fusion
  330.6 2.9 convolution_bitcast_fusion.1
  333.5 7.0 pad_maximum_fusion
  340.5 4.4 all-to-all-start.1
  344.9 5.7 bitcast_add_fusion
  350.6 14.5 %all-to-all-done.1 = f32[4,2,64,768]{3,2,1,0:T(8,128)} async-done(((f32[4,2,64,768]{3,2,1,0:T(8,128)}), f32[4,2,64,768]{3,2,1,0:T(8,128)}, u32[]{:S(2)}, u32[]{:S(2)}) %all-to-all-start.1) | async-done | bytes 1572896 | tf_op jit(solution)/shard_map/all_to_all | solution.py:140
  365.0 4.6 all-to-all-start.3
  371.6 5.4 reduce-scatter.10.cloned.1.call-done
  379.1 3.2 gather_fusion.1
  382.3 7.4 all-to-all-done.3
  389.8 3.2 gather_fusion.3
  393.0 4.0 select_select_fusion
  397.0 146.5 %reduce-scatter.6.cloned.1.call-done = f32[4,96,768]{2,1,0:T(8,128)} async-done(((f32[4,768,768]{2,1,0:T(8,128)}), f32[4,96,768]{2,1,0:T(8,128)}) %reduce-scatter.6.cloned.1.call-update) | async-done | bytes 1179664 | tf_op jit(solution)/shard_map/reduce_scatter | solution.py:241
  545.6 314.0 %reduce-scatter.8.cloned.1.call-done = f32[2,96,3072]{2,1,0:T(8,128)} async-done(((f32[2,768,3072]{2,1,0:T(8,128)}), f32[2,96,3072]{2,1,0:T(8,128)}) %reduce-scatter.8.cloned.1.call-update) | async-done | bytes 2359312 | tf_op jit(solution)/shard_map/reduce_scatter | solution.py:242
  859.7 2.9 fusion.17
  865.1 36.7 %all-reduce.3 = (f32[2,3072]{1,0:T(2,128)}, f32[4,768]{1,0:T(4,128)}, f32[6]{0:T(128)}) all-reduce(f32[2,3072]{1,0:T(2,128)} %get-tuple-element.54, f32[4,768]{1,0:T(4,128)S(1)} %get-tuple-element.60, f32[6]{0:T(128)} %pad_maximum_fusion.5), channel_id=1, replica_groups=mesh['group'=4,'mp'=8] {'mp'}, use_global_device_ids=true, to_apply=%region_32.35 | all-reduce | flops 9222 | bytes 73776 | tf_op jit(solution)/shard_map/psum | solution.py:277
  908.8 17.8 %all-reduce.2 = (f32[4]{0:T(128)}, f32[2]{0:T(128)}, f32[12]{0:T(128)}) all-reduce(f32[4]{0:T(128)} %multiply_reduce_fusion.10, f32[2]{0:T(128)} %multiply_reduce_fusion.2, f32[12]{0:T(128)} %multiply_reduce_fusion.13), channel_id=1, replica_groups=mesh['group'=4,'mp'=8] {'mp'}, use_global_device_ids=true, to_apply=%region_37.40 | all-reduce | flops 18 | bytes 144 | tf_op jit(solution)/shard_map/psum | solution.py:289
  934.6 2.6 fusion.36
  937.3 2.7 fusion.16
  (199 shorter events, 63.2 us)
Async XLA Ops:
  7.2 2.4 copy-start.7
  7.2 86.8 %all-gather.4.cloned.1.call-start = ((), (), s32[]{:S(2)}) async-start(), calls=%async_computation.7 | async-start | bytes 5308416 | tf_op jit(solution)/shard_map/all_gather | solution.py:87
  9.6 223.5 %all-gather.6.cloned.1.call-start = ((), (), s32[]{:S(2)}) async-start(), calls=%async_computation.8 | async-start | bytes 10616832 | tf_op jit(solution)/shard_map/all_gather | solution.py:88
  12.4 1.6 copy-start.34
  12.4 1.6 copy-start.35
  17.8 1.8 copy-start.19
  46.7 35.6 %copy-start = (f32[4,2,64,768]{3,2,1,0:T(8,128)}, f32[4,2,64,768]{3,2,1,0:T(8,128)S(1)}, u32[]{:S(2)}) copy-start(f32[4,2,64,768]{3,2,1,0:T(8,128)S(1)} %all_to_all.20) | copy-start | bytes 4718596
  46.7 3.9 copy-start.31
  46.7 35.7 %all-to-all-start = ((f32[4,2,64,768]{3,2,1,0:T(8,128)}), f32[4,2,64,768]{3,2,1,0:T(8,128)S(1)}, u32[]{:S(2)}, u32[]{:S(2)}) async-start(f32[4,2,64,768]{3,2,1,0:T(8,128)} %bitcast.159), calls=%async_computation | async-start | bytes 3145728 | tf_op jit(solution)/shard_map/all_to_all | solution.py:83
  50.5 326.4 %reduce-scatter.10.cloned.1.call-start = ((), (), s32[]{:S(2)}) async-start(), calls=%async_computation.11 | async-start | bytes 442368
  82.4 15.6 %copy-start.13 = (f32[4,2,64,768]{3,2,1,0:T(8,128)}, f32[4,2,64,768]{3,2,1,0:T(8,128)S(1)}, u32[]{:S(2)}) copy-start(f32[4,2,64,768]{3,2,1,0:T(8,128)S(1)} %all-to-all-done) | copy-start | bytes 4718596
  82.5 15.6 %copy-start.21 = (bf16[512,768]{1,0:T(8,128)(2,1)}, bf16[512,768]{1,0:T(8,128)(2,1)S(1)}, u32[]{:S(2)}) copy-start(bf16[512,768]{1,0:T(8,128)(2,1)S(1)} %bitcast_convert_fusion.1) | copy-start | bytes 2359300
  99.3 2.2 copy-start.25
  102.8 2.9 copy-start.24
  112.5 1.6 copy-start.9
  233.1 20.2 %copy-start.15 = (f32[512,768]{1,0:T(8,128)S(1)}, f32[512,768]{1,0:T(8,128)}, u32[]{:S(2)}) copy-start(f32[512,768]{1,0:T(8,128)} %copy-done.14) | copy-start | bytes 4718596
  233.1 20.2 %copy-start.43 = (bf16[2,768,3072]{2,1,0:T(8,128)(2,1)S(1)}, bf16[2,768,3072]{2,1,0:T(8,128)(2,1)}, u32[]{:S(2)}) copy-start(bf16[2,768,3072]{2,1,0:T(8,128)(2,1)} %all-gather.6.cloned.1.call-done) | copy-start | bytes 28311556
  253.3 2.8 copy-start.20
  256.2 1.4 copy-start.1
  260.0 7.4 copy-start.12
  267.4 3.2 copy-start.44
  283.2 3.3 copy-start.3
  290.1 2.1 copy-start.4
  292.2 1.4 copy-start.18
  292.2 1.6 copy-start.23
  317.2 226.3 %reduce-scatter.6.cloned.1.call-start = ((), (), s32[]{:S(2)}) async-start(), calls=%async_computation.9 | async-start | bytes 10616832 | tf_op jit(solution)/shard_map/reduce_scatter | solution.py:241
  325.3 534.3 %reduce-scatter.8.cloned.1.call-start = ((), (), s32[]{:S(2)}) async-start(), calls=%async_computation.10 | async-start | bytes 21233664 | tf_op jit(solution)/shard_map/reduce_scatter | solution.py:242
  325.4 5.2 copy-start.16
  325.4 5.2 copy-start.45
  340.5 24.5 %all-to-all-start.1 = ((f32[4,2,64,768]{3,2,1,0:T(8,128)}), f32[4,2,64,768]{3,2,1,0:T(8,128)}, u32[]{:S(2)}, u32[]{:S(2)}) async-start(f32[4,2,64,768]{3,2,1,0:T(8,128)} %bitcast.158), calls=%async_computation.1 | async-start | bytes 3145728 | tf_op jit(solution)/shard_map/all_to_all | solution.py:140
  350.5 19.1 %copy-start.33 = (f32[1,6,96]{2,0,1:T(1,128)S(1)}, f32[1,6,96]{2,0,1:T(1,128)}, u32[]{:S(2)}) copy-start(f32[1,6,96]{2,0,1:T(1,128)} %param.23) | copy-start | bytes 6916
  350.5 19.7 %copy-start.30 = (f32[1,9216]{1,0:T(1,128)S(1)}, f32[1,9216]{1,0:T(1,128)}, u32[]{:S(2)}) copy-start(f32[1,9216]{1,0:T(1,128)} %param.24) | copy-start | bytes 110596
  350.5 21.0 %copy-start.40 = (s32[8]{0:T(128)S(1)}, s32[8]{0:T(128)}, u32[]{:S(2)}) copy-start(s32[8]{0:T(128)} %get-tuple-element.85) | copy-start | bytes 100
  350.6 27.9 %copy-start.32 = (f32[1,12,96]{2,0,1:T(1,128)S(1)}, f32[1,12,96]{2,0,1:T(1,128)}, u32[]{:S(2)}) copy-start(f32[1,12,96]{2,0,1:T(1,128)} %param.25) | copy-start | bytes 13828
  365.0 24.7 %all-to-all-start.3 = ((f32[4,2,64,768]{3,2,1,0:T(8,128)}), f32[4,2,64,768]{3,2,1,0:T(8,128)}, u32[]{:S(2)}, u32[]{:S(2)}) async-start(f32[4,2,64,768]{3,2,1,0:T(8,128)} %bitcast.161), calls=%async_computation.3 | async-start | bytes 3145728 | tf_op jit(solution)/shard_map/all_to_all | solution.py:214
  382.3 10.6 %copy-start.10 = (f32[8,64,768]{2,1,0:T(8,128)S(1)}, f32[8,64,768]{2,1,0:T(8,128)}, u32[]{:S(2)}) copy-start(f32[8,64,768]{2,1,0:T(8,128)} %param.16) | copy-start | bytes 4718596
  382.3 10.6 %copy-start.11 = (f32[8,64,768]{2,1,0:T(8,128)S(1)}, f32[8,64,768]{2,1,0:T(8,128)}, u32[]{:S(2)}) copy-start(f32[8,64,768]{2,1,0:T(8,128)} %param.15) | copy-start | bytes 4718596
  382.3 10.6 %copy-start.37 = (pred[8]{0:T(512)(128)(4,1)S(1)}, pred[8]{0:T(512)(128)(4,1)}, u32[]{:S(2)}) copy-start(pred[8]{0:T(512)(128)(4,1)} %get-tuple-element.84) | copy-start | bytes 28
  382.3 10.6 %copy-start.39 = (pred[8]{0:T(512)(128)(4,1)S(1)}, pred[8]{0:T(512)(128)(4,1)}, u32[]{:S(2)}) copy-start(pred[8]{0:T(512)(128)(4,1)} %copy-done.38) | copy-start | bytes 28
  393.0 152.0 %slice-start = ((f32[1,6,96]{2,0,1:T(1,128)}), f32[1,4,96]{2,0,1:T(1,128)S(1)}, s32[]{:S(2)}) async-start(f32[1,6,96]{2,0,1:T(1,128)} %param.23), calls=%async_computation.12 | async-start | bytes 4096 | tf_op jit(solution)/shard_map/slice | solution.py:261
  859.7 45.7 %copy-start.2 = (f32[2,96,3072]{2,1,0:T(8,128)S(1)}, f32[2,96,3072]{2,1,0:T(8,128)}, u32[]{:S(2)}) copy-start(f32[2,96,3072]{2,1,0:T(8,128)} %reduce-scatter.8.cloned.1.call-done) | copy-start | bytes 7077892
  859.7 47.6 %copy-start.6 = (f32[4,96,768]{2,1,0:T(8,128)S(1)}, f32[4,96,768]{2,1,0:T(8,128)}, u32[]{:S(2)}) copy-start(f32[4,96,768]{2,1,0:T(8,128)} %reduce-scatter.6.cloned.1.call-done) | copy-start | bytes 3538948
  902.5 4.7 copy-start.36
  902.6 4.6 copy-start.41
  903.4 2.0 copy-start.27
  926.5 10.7 %copy-start.8 = (f32[1,2,96,3072]{3,2,1,0:T(8,128)S(1)}, f32[1,2,96,3072]{3,2,1,0:T(8,128)}, u32[]{:S(2)}) copy-start(f32[1,2,96,3072]{3,2,1,0:T(8,128)} %param.21) | copy-start | bytes 7077892
  926.5 10.7 %copy-start.28 = (f32[2,3072]{1,0:T(2,128)S(1)}, f32[2,3072]{1,0:T(2,128)}, u32[]{:S(2)}) copy-start(f32[2,3072]{1,0:T(2,128)} %copy-done.27) | copy-start | bytes 73732
  926.6 10.7 %copy-start.42 = (f32[2]{0:T(128)S(1)}, f32[2]{0:T(128)}, u32[]{:S(2)}) copy-start(f32[2]{0:T(128)} %copy-done.41) | copy-start | bytes 28
  (7 other events, 8.1 us)
Sparse Core Ops, SparseCore 0:
  10.8 83.1 all-gather.3
  96.8 136.2 all-gather.5
  317.3 59.5 reduce-scatter.9
  381.0 162.4 reduce-scatter.5
  547.8 311.8 reduce-scatter.7
where the time goes:
time: 958 us; the launch traced here: 947 us
  waiting for transfers between devices  607 us (63%)
  blocking collectives  110 us (11%)
  matrix products  76.6 us (8%)
  local copies, waits for them, and re-layouts  67.6 us (7%)
  other arithmetic  58.2 us (6%)
  between operations  14.8 us (2%)
  starting transfers between devices  13 us (1%)
    reduce_scatter x1, waiting for transfers between devices, body(): lax.psum_scatter(feedforward_grads, 'mp', scatter_dimension=1, tiled=True)  314 us
    reduce_scatter x1, waiting for transfers between devices, body(): lax.psum_scatter(attention_grads, 'mp', scatter_dimension=1, tiled=True)  146 us
    all_gather x1, waiting for transfers between devices, body(): lax.all_gather(feedforward_weights[0].astype(jnp.bfloat16), 'mp', axis=1,...  108 us
    psum x1, blocking collectives, body(): lax.psum((attention_columns, feedforward_columns, row_sums, vector_square...  36.7 us
    all_gather x1, blocking collectives, body(): lax.all_gather(vectors[0].astype(jnp.bfloat16), 'mp', axis=1, tiled=True)  31.1 us
    all_to_all x1, blocking collectives, body(): lax.all_to_all(send_grads, 'group', split_axis=0, concat_axis=0, tiled=True)  24.1 us
    dot_general x1, matrix products, body(): jnp.dot(first_low, feedforward_full[0], preferred_element_type=jnp.float32)  20.2 us
  transfers between devices with their start and end apart: 8, of which 7 were waited for; matrix products, arithmetic and copies ran while one was open for 9% of the time, Pallas kernels for 0%

commit v1 on v0

--- a/solution.py
+++ b/solution.py
@@ -1,6 +1,11 @@
+import functools
+import types
+
 import jax
 import jax.numpy as jnp
 from jax import lax
+from jax.experimental import pallas as pl
+from jax.experimental.pallas import tpu as pltpu
 from jax.sharding import PartitionSpec as P
 
 HEADS = 12
@@ -35,7 +40,7 @@
     return jax.nn.gelu(tensor, approximate=False)
 
 
-def body(
+def generic_body(
     layer_in,
     cotangent,
     target,
@@ -333,6 +338,1385 @@
     )
 
 
+MESH = pl.DeviceIdType.MESH
+ANY = pl.BlockSpec(memory_space=pl.ANY)
+VMEM = pl.BlockSpec(memory_space=pltpu.VMEM)
+SMEM = pl.BlockSpec(memory_space=pltpu.SMEM)
+LANES = 128
+PEERS = 8
+LIMIT = 63 * 1024 * 1024
+D = 768
+FF = 3072
+QKV = 3 * D
+VEC = QKV + D
+WIDE = VEC + LANES
+SEQ = 64
+TOKENS = 512
+HEAD = D // HEADS
+DECAY = 1.0 - STEP ** (-0.8)
+KEEP = 1.0 - DECAY
+
+
+class Spot:
+    def __init__(self):
+        g = lax.axis_index("group")
+        m = lax.axis_index("mp")
+        y, c = lax.div(g, 2), lax.rem(g, 2)
+        z, x = lax.div(m, 2), lax.rem(m, 2)
+        h, zl = lax.div(z, 2), lax.rem(z, 2)
+        self.g, self.m, self.y, self.c, self.x, self.h, self.zl = g, m, y, c, x, h, zl
+        self.home = c == h
+        self.k = y * 2 + h
+        self.r = c * 4 + zl * 2 + x
+        self.across_x = (g, m + 1 - 2 * x)
+        self.across_z = (g, m + 2 - 4 * zl)
+        self.across_core = (g + 1 - 2 * c, m)
+        self.partner = (y * 2 + 1 - c, ((1 - h) * 2 + zl) * 2 + x)
+
+    def shard(self, dc=0, dz=0, dx=0):
+        c = 1 - self.c if dc else self.c
+        zl = 1 - self.zl if dz else self.zl
+        x = 1 - self.x if dx else self.x
+        return c * 4 + zl * 2 + x
+
+    def router(self, n):
+        y = 1 - self.y if n % 2 else self.y
+        h = 1 - self.h if n // 2 else self.h
+        return (y * 2 + self.c, (h * 2 + self.zl) * 2 + self.x), y * 2 + h
+
+    def peer(self, step):
+        m = lax.rem(self.m + step, PEERS)
+        return (self.g, m), m
+
+
+def rows(index, count):
+    if isinstance(index, int):
+        return pl.ds(index * count, count)
+    return pl.ds(pl.multiple_of(index * count, count), count)
+
+
+def remote(src, dst, send, recv, device):
+    return pltpu.make_async_remote_copy(
+        src_ref=src,
+        dst_ref=dst,
+        send_sem=send,
+        recv_sem=recv,
+        device_id=device,
+        device_id_type=MESH,
+    )
+
+
+def greet(devices):
+    barrier = pltpu.get_barrier_semaphore()
+    for device in devices:
+        pl.semaphore_signal(barrier, inc=1, device_id=device, device_id_type=MESH)
+    pl.semaphore_wait(barrier, len(devices))
+
+
+def dot(a, b):
+    return jnp.dot(a, b, preferred_element_type=jnp.float32)
+
+
+def dot_t(a, b):
+    return lax.dot_general(a, b, (((1,), (1,)), ((), ())), preferred_element_type=jnp.float32)
+
+
+def t_dot(a, b):
+    return lax.dot_general(a, b, (((0,), (0,)), ((), ())), preferred_element_type=jnp.float32)
+
+
+def loop(count, step, unroll=1):
+    def turn(i, carry):
+        for n in range(unroll):
+            step(i * unroll + n)
+        return carry
+
+    if count == unroll:
+        turn(0, 0)
+    else:
+        lax.fori_loop(0, count // unroll, turn, 0)
+
+
+def mean_of(value):
+    return jnp.sum(value, axis=-1, keepdims=True) * (1.0 / D)
+
+
+def sum_rows(value):
+    return jnp.sum(value, axis=0, keepdims=True)
+
+
+def placing(target, keep_mask, capacity):
+    count, groups = target.shape[0], capacity.shape[0]
+    aims = [target[s] for s in range(count)]
+    flags = [keep_mask[s] for s in range(count)]
+    limits = [capacity[k] for k in range(groups)]
+    placed = []
+    for s in range(count):
+        rank = jnp.int32(0)
+        for before in range(s):
+            rank = rank + flags[before] * (aims[before] == aims[s]).astype(jnp.int32)
+        placed.append(
+            [
+                (
+                    flags[s]
+                    * (aims[s] == k).astype(jnp.int32)
+                    * (rank == n).astype(jnp.int32)
+                    * (rank < limits[k]).astype(jnp.int32)
+                ).astype(jnp.float32)
+                for k in range(groups)
+                for n in range(SLOTS)
+            ]
+        )
+    return placed
+
+
+class Heads:
+    def __init__(self):
+        row = lax.broadcasted_iota(jnp.int32, (2 * LANES, LANES), 0)
+        col = lax.broadcasted_iota(jnp.int32, (2 * LANES, LANES), 1)
+        self.same = lax.rem(lax.div(row, SEQ), 2) == lax.div(col, SEQ)
+        self.first = col[:LANES] < HEAD
+        lane = lax.broadcasted_iota(jnp.int32, (1, LANES), 1)
+        self.masks = [
+            (lane < HEAD).astype(jnp.float32).astype(jnp.bfloat16),
+            (lane >= HEAD).astype(jnp.float32).astype(jnp.bfloat16),
+        ]
+
+    def stack(self, pair):
+        return jnp.concatenate([pair * mask for mask in self.masks], axis=0)
+
+    def join(self, both):
+        return jnp.where(self.first, both[:LANES], both[LANES:]).astype(jnp.bfloat16)
+
+    def weigh(self, q, k):
+        scores = jnp.where(self.same, dot_t(q, k) * HEAD ** (-0.5), -3.0e38)
+        largest = jnp.max(scores, axis=-1, keepdims=True)
+        shifted = jnp.exp(scores - largest)
+        return shifted / jnp.sum(shifted, axis=-1, keepdims=True)
+
+
+CHUNK = 512
+CHUNKS = FF // CHUNK
+PAIR = 2 * CHUNK
+BASE = CHUNKS * PAIR
+SPANS = tuple((i * PAIR, PAIR) for i in range(CHUNKS)) + (
+    (BASE, D),
+    (BASE + D, D),
+    (BASE + 2 * D, D),
+    (BASE + 3 * D, D + LANES),
+)
+OUT_PIECE, QUERY_PIECE, KEY_PIECE, VALUE_PIECE = range(CHUNKS, CHUNKS + 4)
+PIECES = CHUNKS + 4
+Z_FIRST = (0,)
+RING = 2
+HALF = 384
+SHARD_AT = 2 * LANES
+STAT_F = 4 * FF + 2 * LANES
+STAT_A = 8 * D + 2 * LANES
+ATTENTION_AT = (BASE + D, BASE + 2 * D, BASE + 3 * D, BASE)
+
+
+def forward_phase(spot, r):
+    low, full = jnp.bfloat16, jnp.float32
+    count = r.diag.shape[0]
+    group_count = r.capacity.shape[0]
+    target, keep_mask, capacity, vectors = r.target, r.keep_mask, r.capacity, r.vectors
+    fa, f1, f2, xt, ot, ht, dft, qkv, g, gp = r.fa, r.f1, r.f2, r.xt, r.ot, r.ht, r.dft, r.qkv, r.g, r.gp
+    n1, inv, dr, df, vt, vg, x, dy, o, h1, hb = r.n1, r.inv, r.dr, r.df, r.vt, r.vg, r.x, r.dy, r.o, r.h1, r.hb
+    qb, bu, square, acc, total = r.qb, r.bu, r.square, r.acc, r.total
+    swap_s, swap_r, x_s, x_r, z_s, z_r, d_s, d_r = r.swap_s, r.swap_r, r.x_s, r.x_r, r.z_s, r.z_r, r.d_s, r.d_r
+    c_s, c_r, t_s, t_r, own_sem, keep_sem, load_sem = r.c_s, r.c_r, r.t_s, r.t_r, r.own_sem, r.keep_sem, r.load_sem
+
+    def raw(block):
+        return (n1, dr, h1)[block // 5].at[pl.ds(block % 5 * count, count)]
+
+    def load_weights(block):
+        src = r.wa.at[block] if block < 4 else r.wf.at[block // 4 - 1, :, pl.ds(block % 4 * D, D)]
+        return pltpu.make_async_copy(src, raw(block), load_sem.at[block])
+
+    def load_tokens(src, s):
+        return pltpu.make_async_copy(
+            src.at[pl.ds(s * SEQ, SEQ)], total.at[pl.ds(0, SEQ), pl.ds(s * D, D)], load_sem.at[12 + s]
+        )
+
+    for block in range(4):
+        load_weights(block).start()
+    for s in range(target.shape[0]):
+        load_tokens(r.layer_in, s).start()
+    for block in range(4, 12):
+        load_weights(block).start()
+    square[...] = jnp.zeros(square.shape, full)
+    for row in range(12):
+        square[row : row + 1, pl.ds(0, count)] = vectors[row]
+    acc[pl.ds(SHARD_AT, count), pl.ds(VEC, LANES)] = square[...].T[:count].astype(low)
+    placed = placing(target, keep_mask, capacity)
+    r.greet()
+    firsts, widths, fulls = (0, WIDE, WIDE + FF), (WIDE, FF, FF), (fa, f1, f2)
+    shards = [acc.at[pl.ds(SHARD_AT, count), pl.ds(*span)] for span in zip(firsts, widths)]
+    pieces = range(3)
+    away = jnp.logical_not(spot.home)
+
+    def swap(p):
+        return remote(
+            shards[p], fulls[p].at[rows(spot.m, count)], swap_s.at[p], swap_r.at[p], spot.partner
+        )
+
+    def keep(p):
+        return pltpu.make_async_copy(shards[p], fulls[p].at[rows(spot.r, count)], own_sem.at[p])
+
+    def hop(p, shard, send, recv, device):
+        view = fulls[p].at[rows(shard, count)]
+        return remote(view, view, send, recv, device)
+
+    def over_x(p, shard):
+        return hop(p, shard, x_s.at[p], x_r.at[p], spot.across_x)
+
+    def over_z(p, shard):
+        return hop(p, shard, z_s.at[p], z_r.at[p], spot.across_z)
+
+    def diagonal(p, shard):
+        return hop(p, shard, d_s.at[p], d_r.at[p], spot.across_x)
+
+    def over_core(p, n, shard):
+        return hop(p, shard, c_s.at[p, n], c_r.at[p, n], spot.across_core)
+
+    routed = (x, dy)
+
+    def token(a, n):
+        device, k = spot.router(n)
+        return remote(
+            acc.at[pl.ds(a * LANES, LANES), rows(k, D)],
+            routed[a].at[pl.ds(n * LANES, LANES)],
+            t_s.at[a, n],
+            t_r.at[a, n],
+            device,
+        )
+
+    def token_keep(a):
+        return pltpu.make_async_copy(
+            acc.at[pl.ds(a * LANES, LANES), rows(spot.k, D)],
+            routed[a].at[pl.ds(0, LANES)],
+            keep_sem.at[a],
+        )
+
+    mine = spot.r
+    by_x, by_z, by_both = spot.shard(dx=1), spot.shard(dz=1), spot.shard(dz=1, dx=1)
+
+    def lead(p):
+        over_x(p, mine).start()
+        over_z(p, mine).start()
+        over_core(p, 0, mine).start()
+
+    def lead_home(p):
+        keep(p).wait()
+        lead(p)
+
+    def lead_away(p):
+        hop(p, mine, swap_s.at[p], swap_r.at[p], spot.partner).wait_recv()
+        lead(p)
+
+    def relay(p):
+        over_z(p, by_z).wait_recv()
+        diagonal(p, by_z).start()
+        over_core(p, 2, by_z).start()
+        over_x(p, by_x).wait_recv()
+        over_core(p, 1, by_x).start()
+
+    def finish(p):
+        diagonal(p, by_both).wait_recv()
+        over_core(p, 3, by_both).start()
+
+    def collect_first(p):
+        over_core(p, 0, spot.shard(dc=1)).wait_recv()
+
+    def collect_rest(p):
+        over_core(p, 1, spot.shard(dc=1, dx=1)).wait_recv()
+        over_core(p, 2, spot.shard(dc=1, dz=1)).wait_recv()
+        over_core(p, 3, spot.shard(dc=1, dz=1, dx=1)).wait_recv()
+
+    def cast(p, block):
+        load_weights(block).wait()
+        at = firsts[p] + block % 4 * D
+        acc[pl.ds(SHARD_AT, count), pl.ds(at, D)] = raw(block)[...].astype(low)
+
+    for block in range(4):
+        cast(0, block)
+
+    @pl.when(away)
+    def _():
+        swap(0).start()
+
+    @pl.when(spot.home)
+    def _():
+        keep(0).start()
+
+    for p in (1, 2):
+        for j in range(4):
+            cast(p, p * 4 + j)
+
+        @pl.when(spot.home)
+        def _():
+            lead_home(p - 1)
+            keep(p).start()
+
+    @pl.when(spot.home)
+    def _():
+        lead_home(2)
+
+    def choose(a):
+        def part(n):
+            parts = [total[rows(n, 16), pl.ds(s * D, D)] for s in range(len(placed))]
+            for slot in range(2 * group_count):
+                value = sum(places[slot] * one for places, one in zip(placed, parts))
+                at = pl.multiple_of(a * LANES + slot % 2 * SEQ + n * 16, 16)
+                acc[pl.ds(at, 16), pl.ds(slot // 2 * D, D)] = value.astype(low)
+
+        loop(SEQ // 16, part)
+
+    for s in range(target.shape[0]):
+        load_tokens(r.layer_in, s).wait()
+    choose(0)
+    for s in range(target.shape[0]):
+        load_tokens(r.cotangent, s).start()
+    token_keep(0).start()
+    token(0, 1).start()
+
+    @pl.when(away)
+    def _():
+        lead_away(0)
+        swap(1).start()
+
+    @pl.when(spot.home)
+    def _():
+        relay(0)
+        finish(0)
+
+    collect_first(0)
+    token(0, 2).start()
+    token(0, 3).start()
+    for s in range(target.shape[0]):
+        load_tokens(r.cotangent, s).wait()
+    choose(1)
+    square[...] = jnp.zeros(square.shape, full)
+    for n, part in enumerate((vectors, r.vector_moments, r.row_moments)):
+        for row in range(part.shape[0]):
+            square[row : row + 1, pl.ds(0, count)] = part[row]
+        r.small[n] = square[...].T[:count]
+
+    @pl.when(away)
+    def _():
+        relay(0)
+        finish(0)
+
+    @pl.when(spot.home)
+    def _():
+        relay(1)
+        finish(1)
+
+    def turn(src, dst, i):
+        block = rows(i, LANES)
+        turned = src[block, :].T
+        dst[rows(1 - spot.c, HALF), block] = turned[:HALF]
+        dst[rows(spot.c, HALF), block] = turned[HALF:]
+
+    token_keep(0).wait()
+    token(0, 1).wait_recv()
+    turn(x, xt, 0)
+    turn(x, xt, 1)
+    collect_rest(0)
+    vt[...] = fa[:, pl.ds(VEC, LANES)].astype(full).T[:16]
+    qb[:, pl.ds(0, D)] = vt[0:1]
+    qb[:, pl.ds(D, D)] = jnp.zeros((1, D), full)
+    qb[:, pl.ds(2 * D, D)] = vt[1:2]
+    for i in range(4):
+        bu[:, pl.ds(i * D, D)] = vt[8 + i : 9 + i]
+
+    def project(first, j):
+        cols = rows(j, 256)
+        at = pl.ds(first, 256)
+        qkv[at, cols] = (dot(x[at, :], fa[:, cols]) + qb[:, cols]).astype(low)
+
+    heads = Heads()
+
+    def attend(block, j):
+        at = pl.ds(block * LANES, LANES)
+        q = qkv[at, rows(j, LANES)]
+        k = qkv[at, rows(j + 6, LANES)]
+        v = qkv[at, rows(j + 12, LANES)]
+        weights = heads.weigh(heads.stack(q), k).astype(low)
+        o[at, rows(j, LANES)] = heads.join(dot(weights, v))
+
+    def attend_block(block):
+        def part(n):
+            for j in range(3):
+                attend(block, n * 3 + j)
+
+        loop(2, part)
+
+    loop(QKV // 256, functools.partial(project, 0), 3)
+
+    @pl.when(spot.home)
+    def _():
+        relay(2)
+
+    attend_block(0)
+    attend_block(1)
+
+    @pl.when(spot.home)
+    def _():
+        finish(2)
+
+    token(0, 2).wait_recv()
+    token(0, 3).wait_recv()
+    loop(QKV // 256, functools.partial(project, 256), 3)
+
+    @pl.when(away)
+    def _():
+        lead_away(1)
+        swap(2).start()
+
+    attend_block(2)
+    attend_block(3)
+
+    @pl.when(away)
+    def _():
+        relay(1)
+
+    def attention_out(j):
+        h1[:, rows(j, 256)] = dot(o[...], fa[:, pl.ds(QKV + j * 256, 256)])
+
+    loop(D // 256, attention_out, 3)
+
+    def first_norm(i):
+        for n in range(2):
+            at = pl.ds(pl.multiple_of(i * 64 + n * 32, 32), 32)
+            stream = x[at, :].astype(full) + (h1[at, :] + vt[2:3])
+            center = stream - mean_of(stream)
+            inverse = lax.rsqrt(mean_of(center * center) + epsilon)
+            normed = center * inverse
+            n1[at, :] = normed
+            inv[at, :] = jnp.broadcast_to(inverse, (32, LANES))
+            value = normed * vt[3:4] + vt[4:5]
+            h1[at, :] = value
+            hb[at, :] = value.astype(low)
+
+    loop(TOKENS // 64, first_norm)
+
+    @pl.when(away)
+    def _():
+        lead_away(2)
+        finish(1)
+
+    collect_first(2)
+    token_keep(1).start()
+    for n in (1, 2, 3):
+        token(1, n).start()
+
+    collect_first(1)
+    collect_rest(1)
+
+    def rise(j, dst):
+        dr[:, pl.ds(dst * 256, 256)] = dot(hb[...], f1[:, rows(j, 256)])
+
+    def bend(j, src):
+        cols = rows(j, 256)
+        for i in range(TOKENS // 32):
+            at = pl.ds(i * 32, 32)
+            u = dr[at, pl.ds(src * 256, 256)] + bu[:, cols]
+            below = 0.5 + 0.5 * lax.erf(u * (0.5**0.5))
+            slope = below + u * (jnp.exp(-0.5 * u * u) * 0.3989422804014327)
+            g[at, cols] = (u * below).astype(low)
+            gp[at, cols] = slope.astype(low)
+
+    rise(0, 0)
+
+    def up(t):
+        rise(2 * t + 1, 1)
+        bend(2 * t, 0)
+        rise(lax.rem(2 * t + 2, FF // 256), 0)
+        bend(2 * t + 1, 1)
+
+    def up_some(first):
+        loop(2, lambda t: up(t + first))
+
+    up_some(0)
+
+    @pl.when(away)
+    def _():
+        relay(2)
+
+    up_some(2)
+
+    @pl.when(away)
+    def _():
+        finish(2)
+
+    up_some(4)
+    for i in range(4):
+        if i >= 2:
+            turn(x, xt, i)
+        turn(hb, ht, i)
+        turn(o, ot, i)
+    def down(half):
+        at = rows(half, D // 2)
+        dr[:, at] = dot_t(g[:, pl.ds(0, D)], f2[at, pl.ds(0, D)])
+
+        def more(n):
+            part = rows(n + 1, D)
+            dr[:, at] += dot_t(g[:, part], f2[at, part])
+
+        loop(FF // D - 1, more, 3)
+
+    @pl.when(away)
+    def _():
+        collect_rest(2)
+
+    down(spot.h)
+
+    @pl.when(spot.home)
+    def _():
+        collect_rest(2)
+
+    down(1 - spot.h)
+    token_keep(1).wait()
+    for n in (1, 2, 3):
+        token(1, n).wait_recv()
+    vg[...] = jnp.zeros(vg.shape, full)
+
+    def second_norm(i):
+        sums = []
+        for n in range(4):
+            at = pl.ds(pl.multiple_of(i * LANES + n * 32, 32), 32)
+            stream = h1[at, :] + (dr[at, :] + vt[5:6])
+            center = stream - mean_of(stream)
+            inverse = lax.rsqrt(mean_of(center * center) + epsilon)
+            normed = center * inverse
+            result = (normed * vt[6:7] + vt[7:8]).astype(low)
+            upstream = dy[at, :].astype(full)
+            dy[at, :] = result
+            scaled = upstream * vt[6:7]
+            back = inverse * (scaled - mean_of(scaled) - normed * mean_of(scaled * normed))
+            dr[at, :] = back
+            rounded = back.astype(low)
+            df[at, :] = rounded
+            sums.append((sum_rows(rounded.astype(full)), sum_rows(upstream * normed), sum_rows(upstream)))
+        for row, parts in enumerate(zip(*sums)):
+            vg[5 + row : 6 + row] += sum(parts)
+        turn(df, dft, i)
+
+    loop(TOKENS // LANES, second_norm)
+    for a in (0, 1):
+        for n in (1, 2, 3):
+            token(a, n).wait_send()
+
+    @pl.when(away)
+    def _():
+        for p in pieces:
+            swap(p).wait_send()
+
+    def settle():
+        for p in pieces:
+            over_x(p, mine).wait_send()
+            over_z(p, mine).wait_send()
+            diagonal(p, by_z).wait_send()
+            for n, shard in enumerate((mine, by_x, by_z, by_both)):
+                over_core(p, n, shard).wait_send()
+
+    return settle
+
+
+def backward_phase(spot, r, settle):
+    low, full = jnp.bfloat16, jnp.float32
+    count = r.diag.shape[0]
+    away = jnp.logical_not(spot.home)
+    columns, got_outs, got_grads, sums, by_row, by_column = r.columns, r.got_outs, r.got_grads, r.sums, r.by_row, r.by_column
+    vectors_grad, rows_new, columns_new = r.vectors_grad, r.rows_new, r.columns_new
+    moments_new, vectors_new, scale_new = r.moments_new, r.vectors_new, r.scale_new
+    fa, f1, f2, xt, ot, ht, dft, qkv, g, gp = r.fa, r.f1, r.f2, r.xt, r.ot, r.ht, r.dft, r.qkv, r.g, r.gp
+    n1, inv, dr, df, vt, vg, dbu, vt_low, square = r.n1, r.inv, r.dr, r.df, r.vt, r.vg, r.dbu, r.vt_low, r.square
+    da, do, dx, du = r.x, r.dy, r.o, r.hb
+    acc, other, stage_f, stage_v, total = r.acc, r.other, r.stage_f, r.stage_v, r.total
+    diag, from_x, from_z, swapped = r.diag, r.from_x, r.from_z, r.swapped
+    stf, sta, srf, sra, small, small_new, spread_row = r.stf, r.sta, r.srf, r.sra, r.small, r.small_new, r.square.at[pl.ds(0, count)]
+    out_sem, core_s, core_r, x_s, x_r, z_s, z_r = r.out_sem, r.core_s, r.core_r, r.bx_s, r.bx_r, r.bz_s, r.bz_r
+    d_s, d_r, swap_s, swap_r, st_s, st_r, st_keep = r.bd_s, r.bd_r, r.bswap_s, r.bswap_r, r.st_s, r.st_r, r.st_keep
+    t_s, t_r, keep_sem = r.bt_s, r.bt_r, r.bkeep_sem
+    routed = ((do, got_outs), (dx, got_grads))
+
+    def token(a, n):
+        device, k = spot.router(n)
+        src, dst = routed[a]
+        return remote(
+            src.at[pl.ds(n * LANES, LANES)],
+            dst.at[rows(spot.k, LANES)],
+            t_s.at[a, n],
+            t_r.at[a, n],
+            device,
+        )
+
+    def token_from(a, n):
+        device, k = spot.router(n)
+        src, dst = routed[a]
+        return remote(
+            src.at[pl.ds(n * LANES, LANES)],
+            dst.at[rows(k, LANES)],
+            t_s.at[a, n],
+            t_r.at[a, n],
+            device,
+        )
+
+    def token_keep(a):
+        src, dst = routed[a]
+        return pltpu.make_async_copy(
+            src.at[pl.ds(0, LANES)], dst.at[rows(spot.k, LANES)], keep_sem.at[a]
+        )
+
+    def send_tokens(a, which=(1, 2, 3)):
+        for n in which:
+            token(a, n).start()
+
+    here = spot.zl * 2 + spot.x
+    at_x = spot.zl * 2 + 1 - spot.x
+    at_z = (1 - spot.zl) * 2 + spot.x
+    at_both = (1 - spot.zl) * 2 + 1 - spot.x
+
+    def cols(p):
+        if isinstance(p, int):
+            return pl.ds(*SPANS[p])
+        return rows(p, PAIR)
+
+    def trade(p):
+        if isinstance(p, int) and p >= CHUNKS:
+            first, width = SPANS[p][0], D
+            src = f1.at[pl.ds(0, HALF), pl.ds(first - BASE, width)]
+            dst = other.at[:, pl.ds(first, width)]
+        else:
+            src, dst = stage_f.at[lax.rem(p, RING)], other.at[:, cols(p)]
+        return remote(src, dst, core_s.at[p], core_r.at[p], spot.across_core)
+
+    def trade_vectors():
+        return remote(
+            stage_v,
+            other.at[:, pl.ds(BASE + VEC, LANES)],
+            core_s.at[PIECES],
+            core_r.at[PIECES],
+            spot.across_core,
+        )
+
+    def over_x(p):
+        return remote(
+            acc.at[rows(at_x, count), cols(p)],
+            from_x.at[:, cols(p)],
+            x_s.at[p],
+            x_r.at[p],
+            spot.across_x,
+        )
+
+    def over_z(p):
+        return remote(
+            acc.at[rows(at_z, count), cols(p)],
+            from_z.at[:, cols(p)],
+            z_s.at[p],
+            z_r.at[p],
+            spot.across_z,
+        )
+
+    def diagonal(p, z_first):
+        return remote(
+            acc.at[rows(at_both, count), cols(p)],
+            diag.at[:, cols(p)],
+            d_s.at[p],
+            d_r.at[p],
+            spot.across_z if z_first else spot.across_x,
+        )
+
+    def swap(p):
+        return remote(
+            acc.at[rows(here, count), cols(p)],
+            swapped.at[:, cols(p)],
+            swap_s.at[p],
+            swap_r.at[p],
+            spot.partner,
+        )
+
+    stats, gathered = (stf, sta), (srf, sra)
+
+    def share(n, step):
+        device, _ = spot.peer(step)
+        return remote(stats[n], gathered[n].at[spot.m], st_s.at[n, step], st_r.at[n, step], device)
+
+    def share_from(n, step):
+        device, m = spot.peer((PEERS - step) % PEERS)
+        return remote(stats[n], gathered[n].at[m], st_s.at[n, step], st_r.at[n, step], device)
+
+    def share_keep(n):
+        return pltpu.make_async_copy(stats[n], gathered[n].at[spot.m], st_keep.at[n])
+
+    def meet(p):
+        trade(p).wait_recv()
+        if isinstance(p, int) and p == VALUE_PIECE:
+            trade_vectors().wait_recv()
+
+        def add(i):
+            view = (rows(i, 32), cols(p))
+            acc[view] = acc[view] + other[view]
+
+        loop(HALF // 32, add, 3)
+
+        def forward(z_first):
+            diagonal(p, z_first).start()
+            if z_first:
+                over_z(p).start()
+            else:
+                over_x(p).start()
+
+        forward(isinstance(p, int) and p in Z_FIRST)
+
+    def relay(p):
+        z_first = p in Z_FIRST
+        diagonal(p, z_first).wait_recv()
+        base = at_x if z_first else at_z
+
+        def add(i):
+            view = (pl.ds(pl.multiple_of(base * count + i * 32, 32), 32), cols(p))
+            acc[view] = acc[view] + diag[rows(i, 32), cols(p)]
+
+        loop(count // 32, add, 3)
+        if z_first:
+            over_x(p).start()
+        else:
+            over_z(p).start()
+
+    def close(p):
+        over_x(p).wait_recv()
+        over_z(p).wait_recv()
+
+        def add(i):
+            view = (pl.ds(pl.multiple_of(here * count + i * 16, 16), 16), cols(p))
+            part = (rows(i, 16), cols(p))
+            done = acc[view].astype(full) + from_x[part].astype(full) + from_z[part].astype(full)
+            total[part] = done
+            acc[view] = done.astype(low)
+
+        loop(count // 16, add, 3)
+
+        @pl.when(away)
+        def _():
+            swap(p).start()
+
+    token_keep(0).start()
+    send_tokens(0)
+
+    def chunk(c):
+        third = lax.rem(c, RING)
+        mine = rows(c, CHUNK)
+
+        @pl.when(c >= RING)
+        def _():
+            trade(c - RING).wait_send()
+
+        first = pl.multiple_of(c * PAIR, PAIR)
+
+        def give(left, right, shift, at):
+            def part(n):
+                n = n * 256
+                whole = dot(left[...], right[:, pl.ds(pl.multiple_of(shift + n, 256), 256)]).astype(low)
+                stage_f[third, :, pl.ds(pl.multiple_of(at + n, 256), 256)] = whole[:HALF]
+                acc[:, pl.ds(pl.multiple_of(first + at + n, 256), 256)] = whole[HALF:]
+
+            loop(CHUNK // 256, part, 2)
+
+        def bend_back(i):
+            at, here_c = rows(i, 256), rows(c * 2 + i, 256)
+            value = dot(df[...], f2[:, here_c]) * gp[:, here_c].astype(full)
+            rounded = value.astype(low)
+            du[:, at] = rounded
+            dbu[:, here_c] = sum_rows(rounded.astype(full))
+
+        loop(CHUNK // 256, bend_back, 2)
+        give(dft, g, c * CHUNK, CHUNK)
+
+        @pl.when(c >= 2)
+        def _():
+            meet(c - 1)
+
+        give(ht, du, 0, 0)
+        trade(c).start()
+        def lift(i):
+            at = rows(i, 256)
+            dr[:, at] += dot_t(du[:, pl.ds(0, CHUNK)], f1[at, mine])
+
+        loop(D // 256, lift, 3)
+
+        @pl.when(c == 0)
+        def _():
+            meet(0)
+
+        @pl.when(c == 3)
+        def _():
+            relay(0)
+
+        @pl.when(c == 5)
+        def _():
+            relay(1)
+            close(0)
+
+    loop(CHUNKS, chunk)
+    meet(CHUNKS - 1)
+    for row in range(4):
+        vg[8 + row : 9 + row] = dbu[:, pl.ds(row * D, D)]
+    settle()
+
+    def first_norm_back(i):
+        sums = []
+        for n in range(2):
+            at = pl.ds(pl.multiple_of(i * 64 + n * 32, 32), 32)
+            normed = n1[at, :]
+            upstream = dr[at, :]
+            scaled = upstream * vt[3:4]
+            back = inv[at, :1] * (scaled - mean_of(scaled) - normed * mean_of(scaled * normed))
+            dr[at, :] = back
+            rounded = back.astype(low)
+            da[at, :] = rounded
+            sums.append((sum_rows(rounded.astype(full)), sum_rows(upstream * normed), sum_rows(upstream)))
+        for row, (one, two) in enumerate(zip(*sums)):
+            vg[2 + row : 3 + row] += one + two
+
+    loop(TOKENS // 64, first_norm_back)
+    def outer(src, right, first, j):
+        def part(n):
+            at = n * 256
+            whole = dot(src[...], right[:, pl.ds(j * D + at, 256)]).astype(low)
+            f1[pl.ds(0, HALF), pl.ds(first - BASE + at, 256)] = whole[:HALF]
+            acc[:, pl.ds(first + at, 256)] = whole[HALF:]
+
+        loop(D // 256, part, 3)
+
+    outer(ot, da, BASE, 0)
+    trade(OUT_PIECE).start()
+
+    token_keep(0).wait()
+    for n in (1, 2, 3):
+        token(0, n).wait_send()
+
+    def out_back(j):
+        do[:, rows(j, 256)] = dot_t(da[...], fa[rows(j, 256), pl.ds(QKV, D)]).astype(low)
+
+    loop(D // 256, out_back, 3)
+    relay(2)
+    close(1)
+    heads = Heads()
+
+    def attend_back(block, j):
+        at = rows(block, LANES)
+        q_cols, k_cols, v_cols = rows(j, LANES), rows(j + 6, LANES), rows(j + 12, LANES)
+        q, k, v = heads.stack(qkv[at, q_cols]), qkv[at, k_cols], qkv[at, v_cols]
+        upstream = heads.stack(do[at, q_cols])
+        weights = heads.weigh(q, k)
+        grad_w = dot_t(upstream, v)
+        centered = grad_w - jnp.sum(grad_w * weights, axis=-1, keepdims=True)
+        grad_s = (weights * centered).astype(low)
+        qkv[at, q_cols] = heads.join(dot(grad_s, k) * HEAD ** (-0.5))
+        qkv[at, k_cols] = (t_dot(grad_s, q) * HEAD ** (-0.5)).astype(low)
+        qkv[at, v_cols] = t_dot(weights.astype(low), upstream).astype(low)
+
+    def attend_back_block(block):
+        def part(n):
+            for j in range(3):
+                attend_back(block, n * 3 + j)
+
+        loop(2, part)
+
+    attend_back_block(0)
+    meet(OUT_PIECE)
+    relay(3)
+    attend_back_block(1)
+    close(2)
+    attend_back_block(2)
+    relay(4)
+    close(3)
+    attend_back_block(3)
+    outer(xt, qkv, BASE + D, 0)
+    trade(QUERY_PIECE).start()
+    outer(xt, qkv, BASE + 2 * D, 1)
+    trade(KEY_PIECE).start()
+
+    def bias_sums(i):
+        at = rows(i, LANES)
+        vg[0:1] += sum_rows(qkv[at, pl.ds(0, D)].astype(full))
+        vg[1:2] += sum_rows(qkv[at, pl.ds(2 * D, D)].astype(full))
+
+    loop(4, bias_sums)
+    vt_low[...] = vg[...].T.astype(low)
+    stage_v[...] = vt_low[rows(1 - spot.c, HALF), :]
+    trade_vectors().start()
+    acc[:, pl.ds(BASE + VEC, LANES)] = vt_low[rows(spot.c, HALF), :]
+    outer(xt, qkv, BASE + 3 * D, 2)
+    trade(VALUE_PIECE).start()
+    meet(QUERY_PIECE)
+    relay(5)
+    close(4)
+    meet(KEY_PIECE)
+
+    def input_back(j):
+        at = rows(j, 256)
+
+        value = dr[:, at]
+        for n in range(3):
+            value = value + dot_t(qkv[:, rows(n, D)], fa[at, rows(n, D)])
+        dx[:, at] = value.astype(low)
+
+    loop(D // 256, input_back)
+    token_keep(1).start()
+    send_tokens(1)
+    meet(VALUE_PIECE)
+    lane = lax.broadcasted_iota(jnp.int32, (1, LANES), 1)
+    row_new = {}
+
+    def arrive(p):
+        @pl.when(away)
+        def _():
+            swap(p).wait_recv()
+            total[:, cols(p)] = swapped[:, cols(p)].astype(full)
+
+        put(p).start()
+
+    def put(p):
+        return pltpu.make_async_copy(total.at[:, cols(p)], sums.at[:, cols(p)], out_sem.at[p])
+
+    def tally_feedforward():
+        for c in range(CHUNKS):
+            arrive(c)
+        for w in range(2):
+            spread_row[...] = jnp.zeros(spread_row.shape, full)
+
+            def add_squares(c):
+                at = pl.ds(pl.multiple_of(c * PAIR + w * CHUNK, CHUNK), CHUNK)
+                m = total[:, at]
+                held = m * m + tiny_square
+                spread_row[:, :1] += jnp.sum(held, axis=1, keepdims=True)
+                stf[:, at] = sum_rows(held)
+
+            loop(CHUNKS, add_squares)
+            r = DECAY * small[2, :, 4 + w : 5 + w] + KEEP * (spread_row[:, :1] / FF)
+            row_new[4 + w] = r
+            inverse = 1.0 / r
+
+            def weigh_squares(c):
+                first = pl.multiple_of(c * PAIR + w * CHUNK, CHUNK)
+                m = total[:, pl.ds(first, CHUNK)]
+                stf[:, pl.ds(pl.multiple_of(2 * FF + first, CHUNK), CHUNK)] = sum_rows(m * m * inverse)
+
+            loop(CHUNKS, weigh_squares)
+            stf[:, pl.ds(4 * FF + w * LANES, LANES)] = jnp.broadcast_to(sum_rows(r), (1, LANES))
+        spread(0)
+
+    def spread(n):
+        share_keep(n).start()
+        for step in range(1, PEERS):
+            share(n, step).start()
+
+    row_sums = [jnp.zeros((1, LANES), full)]
+
+    def tally_matrix(j):
+        m = total[:, pl.ds(ATTENTION_AT[j], D)]
+        squared = m * m
+        held = squared + tiny_square
+        mean = jnp.sum(held, axis=1, keepdims=True) / D
+        r = DECAY * small[2, :, j : j + 1] + KEEP * mean
+        row_new[j] = r
+        sta[:, pl.ds(j * D, D)] = sum_rows(held)
+        sta[:, pl.ds((4 + j) * D, D)] = sum_rows(squared * (1.0 / r))
+        row_sums[0] = jnp.where(lane == j, sum_rows(r), row_sums[0])
+
+    def tally_vectors():
+        sta[:, pl.ds(8 * D, LANES)] = row_sums[0]
+        m = total[:, pl.ds(BASE + VEC, LANES)]
+        renewed = DECAY * small[1] + KEEP * (m * m + tiny_square)
+        move = m * lax.rsqrt(renewed)
+        small_new[0] = m
+        small_new[1] = renewed
+        small_new[2] = move
+        sta[:, pl.ds(8 * D + LANES, LANES)] = sum_rows(move * move)
+        spread(1)
+
+    scale = [jnp.zeros((1, LANES), full)]
+
+    def gathered_sum(n, first, width):
+        value = gathered[n][0, :, pl.ds(first, width)]
+        for peer in range(1, PEERS):
+            value = value + gathered[n][peer, :, pl.ds(first, width)]
+        return value
+
+    def take(n):
+        share_keep(n).wait()
+        for step in range(1, PEERS):
+            share_from(n, step).wait_recv()
+
+    def renew(n, index, mean, tiles, column_at, entries):
+        weighted = jnp.zeros((1, 1), full)
+        for at_stat, at_column, width in tiles:
+            here_c = (slice(None), pl.ds(at_column, width))
+            c = DECAY * columns[here_c] + KEEP * (gathered_sum(n, at_stat, width) / D)
+            columns_new[here_c] = c
+            sums = gathered_sum(n, column_at + at_stat, width)
+            weighted = weighted + jnp.sum(sums * mean / c, axis=1, keepdims=True)
+        size = jnp.sqrt(weighted / entries)
+        scale[0] = jnp.where(lane == index, size, scale[0])
+        factor = jnp.sqrt(mean) * (matrix_rate / jnp.maximum(1.0, size / clip_level))
+        for _, at_column, width in tiles:
+            here_c = (slice(None), pl.ds(at_column, width))
+            by_column[here_c] = lax.rsqrt(columns_new[here_c]) * factor
+
+    close(5)
+    relay(OUT_PIECE)
+    relay(QUERY_PIECE)
+    close(OUT_PIECE)
+    relay(KEY_PIECE)
+    tally_feedforward()
+    close(QUERY_PIECE)
+    relay(VALUE_PIECE)
+    arrive(OUT_PIECE)
+    tally_matrix(3)
+    close(KEY_PIECE)
+    arrive(QUERY_PIECE)
+    tally_matrix(0)
+    close(VALUE_PIECE)
+    arrive(KEY_PIECE)
+    tally_matrix(1)
+    take(0)
+    for w in range(2):
+        mean = gathered_sum(0, 4 * FF + w * LANES, LANES)[:, :1] / D
+        tiles = [
+            (c * PAIR + w * CHUNK, 4 * D + w * FF + c * CHUNK, CHUNK) for c in range(CHUNKS)
+        ]
+        renew(0, 4 + w, mean, tiles, 2 * FF, D * FF)
+    arrive(VALUE_PIECE)
+    tally_matrix(2)
+    tally_vectors()
+    take(1)
+    extra = gathered_sum(1, 8 * D, LANES)
+    for j in range(4):
+        renew(1, j, extra[:, j : j + 1] / D, [(j * D, j * D, D)], 4 * D, D * D)
+    size = jnp.sqrt(gathered_sum(1, 8 * D + LANES, LANES) / D)
+    small_new[3] = small[0] - small_new[2] * (vector_rate / jnp.maximum(1.0, size / clip_level))
+    scale_new[...] = jnp.where(lane < 6, scale[0], pltpu.roll(size, 6, 1))[:, : scale_new.shape[1]]
+    row_all = jnp.zeros((count, LANES), full)
+    lanes = lax.broadcasted_iota(jnp.int32, (count, LANES), 1)
+    for j in range(6):
+        row_all = jnp.where(lanes == j, row_new[j], row_all)
+    small_new[2] = row_all
+    by_row[...] = lax.rsqrt(jnp.where(lanes < 6, row_all, 1.0))
+    for n, dst in enumerate((vectors_grad, moments_new, rows_new, vectors_new)):
+        square[pl.ds(0, count), :] = small_new[n]
+        turned = square[...].T
+        for row in range(dst.shape[0]):
+            dst[row] = turned[row : row + 1, :count]
+
+    for p in range(PIECES):
+        if p >= CHUNKS - RING:
+            trade(p).wait_send()
+        diagonal(p, p in Z_FIRST).wait_send()
+        over_x(p).wait_send()
+        over_z(p).wait_send()
+    for n in range(2):
+        for step in range(1, PEERS):
+            share(n, step).wait_send()
+
+    @pl.when(away)
+    def _():
+        for p in range(PIECES):
+            swap(p).wait_send()
+
+    trade_vectors().wait_send()
+    token_keep(1).wait()
+    for n in (1, 2, 3):
+        token_from(0, n).wait_recv()
+        token_from(1, n).wait_recv()
+        token(1, n).wait_send()
+    for p in range(PIECES):
+        put(p).wait()
+
+
+LAYER_IN = (
+    "wa", "wf", "layer_in", "cotangent", "vectors", "row_moments", "vector_moments", "columns", "target", "keep_mask",
+    "capacity",
+)
+LAYER_OUT = (
+    "got_outs", "got_grads", "sums", "by_row", "by_column", "vectors_grad", "rows_new", "columns_new", "moments_new",
+    "vectors_new", "scale_new",
+)
+
+
+def layer_scratch(count):
+    low, full = jnp.bfloat16, jnp.float32
+    wide = BASE + WIDE
+    dma = pltpu.SemaphoreType.DMA
+    buffers = dict(
+        fa=((D, WIDE), low),
+        f1=((D, FF), low),
+        f2=((D, FF), low),
+        xt=((D, TOKENS), low),
+        ot=((D, TOKENS), low),
+        ht=((D, TOKENS), low),
+        dft=((D, TOKENS), low),
+        qkv=((TOKENS, QKV), low),
+        g=((TOKENS, FF), low),
+        gp=((TOKENS, FF), low),
+        n1=((TOKENS, D), full),
+        inv=((TOKENS, LANES), full),
+        dr=((TOKENS, D), full),
+        df=((TOKENS, D), low),
+        vt=((16, D), full),
+        vg=((LANES, D), full),
+        x=((TOKENS, D), low),
+        dy=((TOKENS, D), low),
+        o=((TOKENS, D), low),
+        h1=((TOKENS, D), full),
+        hb=((TOKENS, D), low),
+        qb=((1, QKV), full),
+        bu=((1, FF), full),
+        square=((LANES, LANES), full),
+        dbu=((1, FF), full),
+        vt_low=((D, LANES), low),
+        acc=((HALF, wide), low),
+        other=((HALF, wide), low),
+        stage_f=((RING, HALF, PAIR), low),
+        stage_v=((HALF, LANES), low),
+        diag=((count, wide), low),
+        from_x=((count, wide), low),
+        from_z=((count, wide), low),
+        swapped=((count, wide), low),
+        total=((count, wide), full),
+        stf=((1, STAT_F), full),
+        sta=((1, STAT_A), full),
+        srf=((PEERS, 1, STAT_F), full),
+        sra=((PEERS, 1, STAT_A), full),
+        small=((3, count, LANES), full),
+        small_new=((4, count, LANES), full),
+    )
+    scratch = {name: pltpu.VMEM(*one) for name, one in buffers.items()}
+    for name in ("swap", "x", "z", "d"):
+        for end in ("s", "r"):
+            scratch[f"{name}_{end}"] = dma((3,))
+            scratch[f"b{name}_{end}"] = dma((PIECES,))
+    for end in ("s", "r"):
+        scratch[f"c_{end}"] = dma((3, 4))
+        scratch[f"t_{end}"] = dma((2, 4))
+        scratch[f"bt_{end}"] = dma((2, 4))
+        scratch[f"core_{end}"] = dma((PIECES + 1,))
+        scratch[f"st_{end}"] = dma((2, PEERS))
+    scratch.update(
+        own_sem=dma((3,)), keep_sem=dma((2,)), bkeep_sem=dma((2,)), load_sem=dma((20,)),
+        out_sem=dma((PIECES,)), st_keep=dma((2,)),
+    )
+    return scratch
+
+
+def layer_kernel(names, *refs):
+    r = types.SimpleNamespace(**dict(zip(names, refs)))
+    spot = Spot()
+    r.greet = lambda: greet(
+        [spot.across_core, spot.partner]
+        + [spot.router(n)[0] for n in (1, 2, 3)]
+        + [spot.peer(step)[0] for step in range(1, PEERS)]
+    )
+    settle = forward_phase(spot, r)
+    backward_phase(spot, r, settle)
+
+
+def layer(wa, wf, layer_in, cotangent, vectors, row_moments, vector_moments, columns, *routing):
+    low, full = jnp.bfloat16, jnp.float32
+    count = wa.shape[1]
+    sds = jax.ShapeDtypeStruct
+    scratch = layer_scratch(count)
+    return pl.pallas_call(
+        functools.partial(layer_kernel, LAYER_IN + LAYER_OUT + tuple(scratch)),
+        out_shape=(
+            sds((TOKENS, D), low),
+            sds((TOKENS, D), low),
+            sds((count, BASE + WIDE), full),
+            sds((count, LANES), full),
+            sds(columns.shape, full),
+            sds(vectors.shape, full),
+            sds(row_moments.shape, full),
+            sds(columns.shape, full),
+            sds(vectors.shape, full),
+            sds(vectors.shape, full),
+            sds((1, 18), full),
+        ),
+        in_specs=[ANY] * 4 + [VMEM] * 4 + [SMEM] * 3,
+        out_specs=(ANY,) * 3 + (VMEM,) * 8,
+        scratch_shapes=list(scratch.values()),
+        compiler_params=pltpu.CompilerParams(
+            collective_id=0, has_side_effects=True, vmem_limit_bytes=LIMIT
+        ),
+        name="layer",
+    )(wa, wf, layer_in, cotangent, vectors, row_moments, vector_moments, columns, *routing)
+
+
+WIDTH = 1024
+
+
+def finish_kernel(
+    target, keep_mask, capacity, outs, grads, layer_in, cotangent, sums_f, sums_a, wa, wf, by_row, by_f1, by_f2, by_a,
+    vectors_grad_i, rows_i, columns_i, moments_i, vectors_i, scale_i,
+    layer_out, input_grad, ga, gf, ua, uf, vectors_grad, rows_new, columns_new, moments_new, vectors_new, scale,
+):
+    step = pl.program_id(0)
+    for n in range(2):
+        at = step * 2 + n
+        aim = target[at]
+        rank = jnp.int32(0)
+        for s in range(target.shape[0]):
+            same = (target[s] == aim) & (keep_mask[s] == 1) & (s < at)
+            rank = rank + same.astype(jnp.int32)
+        taken = (keep_mask[at] == 1) & (rank < capacity[aim])
+        slot = jnp.where(taken, aim * SLOTS + rank, 0)
+        here = pl.ds(n * SEQ, SEQ)
+        for src, own, dst in ((outs, layer_in, layer_out), (grads, cotangent, input_grad)):
+            back = src[rows(slot, SEQ), :].astype(jnp.float32)
+            dst[here, :] = jnp.where(taken, back, own[here, :])
+
+    @pl.when(step < FF // WIDTH)
+    def _():
+        for w, by_column in enumerate((by_f1, by_f2)):
+            for n in range(WIDTH // CHUNK):
+                at = pl.ds(n * CHUNK, CHUNK)
+                m = sums_f[:, pl.ds((2 * n + w) * CHUNK, CHUNK)]
+                gf[w, :, at] = m
+                uf[w, :, at] = wf[w, :, at] - m * by_row[:, 4 + w : 5 + w] * by_column[:, at]
+
+    for j in range(4):
+
+        @pl.when(step == j)
+        def _():
+            m = sums_a[...]
+            ga[0] = m
+            ua[0] = wa[0] - m * by_row[:, j : j + 1] * by_a[...]
+
+    @pl.when(step == 0)
+    def _():
+        for src, dst in (
+            (vectors_grad_i, vectors_grad),
+            (rows_i, rows_new),
+            (columns_i, columns_new),
+            (moments_i, moments_new),
+            (vectors_i, vectors_new),
+            (scale_i, scale),
+        ):
+            dst[...] = src[...]
+
+
+def finish(routing, layer_in, cotangent, wa, wf, results):
+    got_outs, got_grads, sums, by_row, by_column, *small = results
+    count = wa.shape[1]
+    full = jnp.float32
+
+    def whole(value):
+        return pl.BlockSpec(value.shape, lambda i: (0,) * len(value.shape))
+
+    def tokens():
+        return pl.BlockSpec((2 * SEQ, D), lambda i: (i, 0))
+
+    def matrix():
+        return pl.BlockSpec((1, count, D), lambda i: (jnp.minimum(i, 3), 0, 0))
+
+    def chunk():
+        return pl.BlockSpec((2, count, WIDTH), lambda i: (0, 0, third(i)))
+
+    def third(i):
+        return jnp.minimum(i, FF // WIDTH - 1)
+
+    def column_block(shape, first):
+        return pl.BlockSpec(shape, lambda i: (0, first // WIDTH + third(i)))
+
+    return pl.pallas_call(
+        finish_kernel,
+        grid=(TOKENS // SEQ // 2,),
+        out_shape=(
+            jax.ShapeDtypeStruct((TOKENS, D), full),
+            jax.ShapeDtypeStruct((TOKENS, D), full),
+            jax.ShapeDtypeStruct(wa.shape, full),
+            jax.ShapeDtypeStruct(wf.shape, full),
+            jax.ShapeDtypeStruct(wa.shape, full),
+            jax.ShapeDtypeStruct(wf.shape, full),
+        )
+        + tuple(jax.ShapeDtypeStruct(one.shape, full) for one in small),
+        in_specs=[SMEM] * 3
+        + [
+            whole(got_outs),
+            whole(got_grads),
+            tokens(),
+            tokens(),
+            pl.BlockSpec((count, 2 * WIDTH), lambda i: (0, third(i))),
+            pl.BlockSpec((count, D), lambda i: (0, BASE // D + lax.rem(jnp.minimum(i, 3) + 1, 4))),
+            matrix(),
+            chunk(),
+            whole(by_row),
+            column_block((1, WIDTH), 4 * D),
+            column_block((1, WIDTH), 4 * D + FF),
+            pl.BlockSpec((1, D), lambda i: (0, jnp.minimum(i, 3))),
+        ]
+        + [whole(one) for one in small],
+        out_specs=(tokens(), tokens(), matrix(), chunk(), matrix(), chunk())
+        + tuple(whole(one) for one in small),
+        compiler_params=pltpu.CompilerParams(vmem_limit_bytes=LIMIT),
+        name="finish",
+    )(
+        *routing, got_outs, got_grads, layer_in, cotangent, sums, sums, wa, wf, by_row, by_column,
+        by_column, by_column, *small,
+    )
+
+def fast_body(
+    layer_in,
+    cotangent,
+    target,
+    keep_mask,
+    capacity,
+    attention_weights,
+    feedforward_weights,
+    vectors,
+    row_moments,
+    column_moments,
+    vector_moments,
+):
+    inputs, upstream = layer_in.reshape(TOKENS, D), cotangent.reshape(TOKENS, D)
+    routing = (target, keep_mask, capacity)
+    vectors, row_moments, vector_moments = (
+        value.transpose(1, 0, 2) for value in (vectors, row_moments, vector_moments)
+    )
+    results = layer(
+        attention_weights[0],
+        feedforward_weights[0],
+        inputs,
+        upstream,
+        vectors,
+        row_moments,
+        vector_moments,
+        column_moments,
+        *routing,
+    )
+    layer_out, input_grad, ga, gf, ua, uf, vectors_grad, rows_new, columns_new, moments_new, vectors_new, scale = finish(
+        routing, inputs, upstream, attention_weights[0], feedforward_weights[0], results
+    )
+    layer_out, input_grad = (value.reshape(layer_in.shape) for value in (layer_out, input_grad))
+    return (
+        layer_out,
+        input_grad,
+        ga[None],
+        gf[None],
+        vectors_grad.transpose(1, 0, 2),
+        rows_new.transpose(1, 0, 2),
+        columns_new,
+        moments_new.transpose(1, 0, 2),
+        ua[None],
+        uf[None],
+        vectors_new.transpose(1, 0, 2),
+        scale,
+    )
+
+
 def solution(mesh):
     in_specs = (
         P(("group", "mp"), None, None),
@@ -361,4 +1745,6 @@
         P("group", None, "mp"),
         P("group", None),
     )
+    suited = mesh.shape["group"] == 4 and mesh.shape["mp"] == PEERS
+    body = fast_body if suited else generic_body
     return jax.shard_map(body, mesh=mesh, in_specs=in_specs, out_specs=out_specs, check_vma=False)

time: 958 us -> 243 us (0.25); the launches traced: 947 us -> 243 us
  waiting for transfers between devices: 607 us -> 0 us
  Pallas kernels: 0 us -> 242 us
  blocking collectives: 110 us -> 0 us
  matrix products: 76.6 us -> 0 us
  local copies, waits for them, and re-layouts: 67.6 us -> 0 us
  other arithmetic: 58.2 us -> 0 us
  between operations: 14.8 us -> 0.83 us
  starting transfers between devices: 13 us -> 0 us
    reduce_scatter x2 -> x0, waiting for transfers between devices: 461 us -> none  [the longest x1 314 us: body(): lax.psum_scatter(feedforward_grads, 'mp', scatter_dimension=1, tiled=True)]
    pallas_call x0 -> x2, Pallas kernels: none -> 242 us  [the longest x1 232 us: layer(): pl.pallas_call(functools.partial(layer_kernel, LAYER_IN + LAYER_OUT + tup...]
    all_gather x2 -> x0, waiting for transfers between devices: 119 us -> none  [the longest x1 108 us: body(): lax.all_gather(feedforward_weights[0].astype(jnp.bfloat16), 'mp', axis=1,...]
    dot_general x18 -> x0, matrix products: 76.6 us -> none  [the longest x1 20.2 us: body(): jnp.dot(first_low, feedforward_full[0], preferred_element_type=jnp.float32)]
    psum x2 -> x0, blocking collectives: 54.5 us -> none  [the longest x1 36.7 us: body(): lax.psum((attention_columns, feedforward_columns, row_sums, vector_square...]
    all_gather x1 -> x0, blocking collectives: 31.1 us -> none  [body(): lax.all_gather(vectors[0].astype(jnp.bfloat16), 'mp', axis=1, tiled=True)]
    all_to_all x1 -> x0, blocking collectives: 24.1 us -> none  [body(): lax.all_to_all(send_grads, 'group', split_axis=0, concat_axis=0, tiled=True)]
    another operation x19 -> x0, local copies, waits for them, and re-layouts: 23.3 us -> none  [the longest x7 12.7 us: body(): jnp.stack([grad_queries.reshape(row_total, model_width), grad_keys.reshap...]
  transfers between devices with their start and end apart: 8 -> 0, of which waited for: 7 -> 0; matrix products, arithmetic and copies ran while one was open for 9% -> 0% of each run, Pallas kernels for 0% -> 0%
where the time goes in v1:
time: 243 us
  Pallas kernels  242 us (100%)
    pallas_call x1, Pallas kernels, layer(): pl.pallas_call(functools.partial(layer_kernel, LAYER_IN + LAYER_OUT + tup...  232 us
    pallas_call x1, Pallas kernels, finish(): pl.pallas_call(finish_kernel, grid=(TOKENS // SEQ // 2,), out_shape=(jax....  9.41 us

profile of v1, /device:TPU:0, one launch (start us, length us, event | category | flops | bytes accessed | tf_op | source)
XLA Modules:
  0.0 242.6 jit_solution(4799726189366063300)
XLA Ops:
  0.6 232.3 %layer.1 = (bf16[512,768]{1,0:T(8,128)(2,1)}, bf16[512,768]{1,0:T(8,128)(2,1)}, f32[96,9344]{1,0:T(8,128)}, f32[96,128]{1,0:T(8,128)}, f32[1,9216]{1,0:T(1,128)}...) custom-call(f32[4,96,768]{2,1,0:T(8,128)} %bitcast.23, ...), custom_call_target="tpu_custom_call" | custom-call | tf_op jit(solution)/shard_map/layer/pallas_call | solution.py:1533
  233.0 9.4 %finish.1 = (f32[512,768]{1,0:T(8,128)}, f32[512,768]{1,0:T(8,128)}, f32[4,96,768]{2,1,0:T(8,128)}, f32[2,96,3072]{2,1,0:T(8,128)}, f32[4,96,768]{2,1,0:T(8,128)...) custom-call(s32[8]{0:T(128)} %target.1, ...), custom_call_target="tpu_custom_call" | custom-call | tf_op jit(solution)/shard_map/finish/pallas_call | solution.py:1634

commit v2 on v1

--- a/solution.py
+++ b/solution.py
@@ -499,15 +499,17 @@
 CHUNKS = FF // CHUNK
 PAIR = 2 * CHUNK
 BASE = CHUNKS * PAIR
-SPANS = tuple((i * PAIR, PAIR) for i in range(CHUNKS)) + (
+SPANS = ((CHUNK, CHUNK),) + tuple((i * PAIR, PAIR) for i in range(1, CHUNKS)) + (
     (BASE, D),
     (BASE + D, D),
     (BASE + 2 * D, D),
     (BASE + 3 * D, D + LANES),
+    (0, CHUNK),
 )
 OUT_PIECE, QUERY_PIECE, KEY_PIECE, VALUE_PIECE = range(CHUNKS, CHUNKS + 4)
-PIECES = CHUNKS + 4
-Z_FIRST = (0,)
+UP_PIECE = CHUNKS + 4
+PIECES = CHUNKS + 5
+Z_FIRST = (UP_PIECE,)
 RING = 2
 HALF = 384
 SHARD_AT = 2 * LANES
@@ -809,9 +811,7 @@
 
     collect_first(2)
     token_keep(1).start()
-    for n in (1, 2, 3):
-        token(1, n).start()
-
+    token(1, 1).start()
     collect_first(1)
     collect_rest(1)
 
@@ -845,6 +845,8 @@
     def _():
         relay(2)
 
+    token(1, 2).start()
+    token(1, 3).start()
     up_some(2)
 
     @pl.when(away)
@@ -879,8 +881,7 @@
 
     down(1 - spot.h)
     token_keep(1).wait()
-    for n in (1, 2, 3):
-        token(1, n).wait_recv()
+    token(1, 1).wait_recv()
     vg[...] = jnp.zeros(vg.shape, full)
 
     def second_norm(i):
@@ -904,7 +905,10 @@
             vg[5 + row : 6 + row] += sum(parts)
         turn(df, dft, i)
 
-    loop(TOKENS // LANES, second_norm)
+    loop(2, second_norm)
+    token(1, 2).wait_recv()
+    token(1, 3).wait_recv()
+    loop(2, lambda i: second_norm(i + 2))
     for a in (0, 1):
         for n in (1, 2, 3):
             token(a, n).wait_send()
@@ -986,7 +990,9 @@
         return rows(p, PAIR)
 
     def trade(p):
-        if isinstance(p, int) and p >= CHUNKS:
+        if isinstance(p, int) and p in (0, UP_PIECE):
+            src, dst = stage_f.at[0, :, pl.ds(*SPANS[p])], other.at[:, cols(p)]
+        elif isinstance(p, int) and p >= CHUNKS:
             first, width = SPANS[p][0], D
             src = f1.at[pl.ds(0, HALF), pl.ds(first - BASE, width)]
             dst = other.at[:, pl.ds(first, width)]
@@ -1111,7 +1117,12 @@
         third = lax.rem(c, RING)
         mine = rows(c, CHUNK)
 
-        @pl.when(c >= RING)
+        @pl.when(c == RING)
+        def _():
+            trade(0).wait_send()
+            trade(UP_PIECE).wait_send()
+
+        @pl.when(c > RING)
         def _():
             trade(c - RING).wait_send()
 
@@ -1133,15 +1144,31 @@
             du[:, at] = rounded
             dbu[:, here_c] = sum_rows(rounded.astype(full))
 
+        give(dft, g, c * CHUNK, CHUNK)
+
+        @pl.when(c == 0)
+        def _():
+            trade(0).start()
+
         loop(CHUNK // 256, bend_back, 2)
-        give(dft, g, c * CHUNK, CHUNK)
+
+        @pl.when(c == 0)
+        def _():
+            meet(0)
 
         @pl.when(c >= 2)
         def _():
             meet(c - 1)
 
         give(ht, du, 0, 0)
-        trade(c).start()
+
+        @pl.when(c == 0)
+        def _():
+            trade(UP_PIECE).start()
+
+        @pl.when(c > 0)
+        def _():
+            trade(c).start()
         def lift(i):
             at = rows(i, 256)
             dr[:, at] += dot_t(du[:, pl.ds(0, CHUNK)], f1[at, mine])
@@ -1150,16 +1177,21 @@
 
         @pl.when(c == 0)
         def _():
-            meet(0)
+            meet(UP_PIECE)
+
+        @pl.when(c == 2)
+        def _():
+            relay(0)
 
         @pl.when(c == 3)
         def _():
-            relay(0)
+            relay(UP_PIECE)
 
         @pl.when(c == 5)
         def _():
             relay(1)
             close(0)
+            close(UP_PIECE)
 
     loop(CHUNKS, chunk)
     meet(CHUNKS - 1)
@@ -1285,6 +1317,7 @@
         return pltpu.make_async_copy(total.at[:, cols(p)], sums.at[:, cols(p)], out_sem.at[p])
 
     def tally_feedforward():
+        arrive(UP_PIECE)
         for c in range(CHUNKS):
             arrive(c)
         for w in range(2):
@@ -1414,7 +1447,7 @@
             dst[row] = turned[row : row + 1, :count]
 
     for p in range(PIECES):
-        if p >= CHUNKS - RING:
+        if CHUNKS - RING <= p < UP_PIECE:
             trade(p).wait_send()
         diagonal(p, p in Z_FIRST).wait_send()
         over_x(p).wait_send()

time: 243 us -> 239 us (0.984)
  Pallas kernels: 242 us -> 238 us
    pallas_call x1, Pallas kernels: 232 us -> 228 us  [layer(): pl.pallas_call(functools.partial(layer_kernel, LAYER_IN + LAYER_OUT + tup...]
where the time goes in v2:
time: 239 us
  Pallas kernels  238 us (100%)
    pallas_call x1, Pallas kernels, layer(): pl.pallas_call(functools.partial(layer_kernel, LAYER_IN + LAYER_OUT + tup...  228 us
    pallas_call x1, Pallas kernels, finish(): pl.pallas_call(finish_kernel, grid=(TOKENS // SEQ // 2,), out_shape=(jax....  9.41 us

profile of v2, /device:TPU:0, one launch (start us, length us, event | category | flops | bytes accessed | tf_op | source)
XLA Modules:
  0.0 238.5 jit_solution(17713253148611128919)
XLA Ops:
  0.6 228.3 %layer.1 = (bf16[512,768]{1,0:T(8,128)(2,1)}, bf16[512,768]{1,0:T(8,128)(2,1)}, f32[96,9344]{1,0:T(8,128)}, f32[96,128]{1,0:T(8,128)}, f32[1,9216]{1,0:T(1,128)}...) custom-call(f32[4,96,768]{2,1,0:T(8,128)} %bitcast.23, ...), custom_call_target="tpu_custom_call" | custom-call | tf_op jit(solution)/shard_map/layer/pallas_call | solution.py:1566
  228.9 9.4 %finish.1 = (f32[512,768]{1,0:T(8,128)}, f32[512,768]{1,0:T(8,128)}, f32[4,96,768]{2,1,0:T(8,128)}, f32[2,96,3072]{2,1,0:T(8,128)}, f32[4,96,768]{2,1,0:T(8,128)...) custom-call(s32[8]{0:T(128)} %target.1, ...), custom_call_target="tpu_custom_call" | custom-call | tf_op jit(solution)/shard_map/finish/pallas_call | solution.py:1667

commit v3 on v2

--- a/solution.py
+++ b/solution.py
@@ -503,18 +503,19 @@
     (BASE, D),
     (BASE + D, D),
     (BASE + 2 * D, D),
-    (BASE + 3 * D, D + LANES),
+    (BASE + 3 * D, 512),
+    (BASE + 3 * D + 512, 256 + LANES),
     (0, CHUNK),
 )
-OUT_PIECE, QUERY_PIECE, KEY_PIECE, VALUE_PIECE = range(CHUNKS, CHUNKS + 4)
-UP_PIECE = CHUNKS + 4
-PIECES = CHUNKS + 5
+OUT_PIECE, QUERY_PIECE, KEY_PIECE, VALUE_PIECE, LAST_PIECE, UP_PIECE = range(CHUNKS, CHUNKS + 6)
+PIECES = CHUNKS + 6
 Z_FIRST = (UP_PIECE,)
 RING = 2
 HALF = 384
 SHARD_AT = 2 * LANES
 STAT_F = 4 * FF + 2 * LANES
-STAT_A = 8 * D + 2 * LANES
+STAT_A = 6 * D + LANES
+STAT_V = 2 * D + 2 * LANES
 ATTENTION_AT = (BASE + D, BASE + 2 * D, BASE + 3 * D, BASE)
 
 
@@ -993,7 +994,8 @@
         if isinstance(p, int) and p in (0, UP_PIECE):
             src, dst = stage_f.at[0, :, pl.ds(*SPANS[p])], other.at[:, cols(p)]
         elif isinstance(p, int) and p >= CHUNKS:
-            first, width = SPANS[p][0], D
+            first, width = SPANS[p]
+            width = min(width, BASE + VEC - first)
             src = f1.at[pl.ds(0, HALF), pl.ds(first - BASE, width)]
             dst = other.at[:, pl.ds(first, width)]
         else:
@@ -1045,7 +1047,7 @@
             spot.partner,
         )
 
-    stats, gathered = (stf, sta), (srf, sra)
+    stats, gathered = (stf, sta, r.stv), (srf, sra, r.srv)
 
     def share(n, step):
         device, _ = spot.peer(step)
@@ -1060,7 +1062,7 @@
 
     def meet(p):
         trade(p).wait_recv()
-        if isinstance(p, int) and p == VALUE_PIECE:
+        if isinstance(p, int) and p == LAST_PIECE:
             trade_vectors().wait_recv()
 
         def add(i):
@@ -1215,14 +1217,15 @@
             vg[2 + row : 3 + row] += one + two
 
     loop(TOKENS // 64, first_norm_back)
-    def outer(src, right, first, j):
+    def outer(src, right, first, j, parts=(0, 1, 2)):
         def part(n):
             at = n * 256
             whole = dot(src[...], right[:, pl.ds(j * D + at, 256)]).astype(low)
             f1[pl.ds(0, HALF), pl.ds(first - BASE + at, 256)] = whole[:HALF]
             acc[:, pl.ds(first + at, 256)] = whole[HALF:]
 
-        loop(D // 256, part, 3)
+        for n in parts:
+            part(n)
 
     outer(ot, da, BASE, 0)
     trade(OUT_PIECE).start()
@@ -1283,8 +1286,10 @@
     stage_v[...] = vt_low[rows(1 - spot.c, HALF), :]
     trade_vectors().start()
     acc[:, pl.ds(BASE + VEC, LANES)] = vt_low[rows(spot.c, HALF), :]
-    outer(xt, qkv, BASE + 3 * D, 2)
+    outer(xt, qkv, BASE + 3 * D, 2, (0, 1))
     trade(VALUE_PIECE).start()
+    outer(xt, qkv, BASE + 3 * D, 2, (2,))
+    trade(LAST_PIECE).start()
     meet(QUERY_PIECE)
     relay(5)
     close(4)
@@ -1302,6 +1307,7 @@
     token_keep(1).start()
     send_tokens(1)
     meet(VALUE_PIECE)
+    meet(LAST_PIECE)
     lane = lax.broadcasted_iota(jnp.int32, (1, LANES), 1)
     row_new = {}
 
@@ -1331,9 +1337,9 @@
                 stf[:, at] = sum_rows(held)
 
             loop(CHUNKS, add_squares)
-            r = DECAY * small[2, :, 4 + w : 5 + w] + KEEP * (spread_row[:, :1] / FF)
-            row_new[4 + w] = r
-            inverse = 1.0 / r
+            moments = DECAY * small[2, :, 4 + w : 5 + w] + KEEP * (spread_row[:, :1] / FF)
+            row_new[4 + w] = moments
+            inverse = 1.0 / moments
 
             def weigh_squares(c):
                 first = pl.multiple_of(c * PAIR + w * CHUNK, CHUNK)
@@ -1341,7 +1347,7 @@
                 stf[:, pl.ds(pl.multiple_of(2 * FF + first, CHUNK), CHUNK)] = sum_rows(m * m * inverse)
 
             loop(CHUNKS, weigh_squares)
-            stf[:, pl.ds(4 * FF + w * LANES, LANES)] = jnp.broadcast_to(sum_rows(r), (1, LANES))
+            stf[:, pl.ds(4 * FF + w * LANES, LANES)] = jnp.broadcast_to(sum_rows(moments), (1, LANES))
         spread(0)
 
     def spread(n):
@@ -1351,27 +1357,27 @@
 
     row_sums = [jnp.zeros((1, LANES), full)]
 
-    def tally_matrix(j):
+    def tally_matrix(j, st, at, count_in):
         m = total[:, pl.ds(ATTENTION_AT[j], D)]
         squared = m * m
         held = squared + tiny_square
         mean = jnp.sum(held, axis=1, keepdims=True) / D
-        r = DECAY * small[2, :, j : j + 1] + KEEP * mean
-        row_new[j] = r
-        sta[:, pl.ds(j * D, D)] = sum_rows(held)
-        sta[:, pl.ds((4 + j) * D, D)] = sum_rows(squared * (1.0 / r))
-        row_sums[0] = jnp.where(lane == j, sum_rows(r), row_sums[0])
+        moments = DECAY * small[2, :, j : j + 1] + KEEP * mean
+        row_new[j] = moments
+        st[:, pl.ds(at * D, D)] = sum_rows(held)
+        st[:, pl.ds((count_in + at) * D, D)] = sum_rows(squared * (1.0 / moments))
+        row_sums[0] = jnp.where(lane == at, sum_rows(moments), row_sums[0])
+        if at == count_in - 1:
+            st[:, pl.ds(2 * count_in * D, LANES)] = row_sums[0]
 
     def tally_vectors():
-        sta[:, pl.ds(8 * D, LANES)] = row_sums[0]
         m = total[:, pl.ds(BASE + VEC, LANES)]
         renewed = DECAY * small[1] + KEEP * (m * m + tiny_square)
         move = m * lax.rsqrt(renewed)
         small_new[0] = m
         small_new[1] = renewed
         small_new[2] = move
-        sta[:, pl.ds(8 * D + LANES, LANES)] = sum_rows(move * move)
-        spread(1)
+        r.stv[:, pl.ds(2 * D + LANES, LANES)] = sum_rows(move * move)
 
     scale = [jnp.zeros((1, LANES), full)]
 
@@ -1410,13 +1416,16 @@
     close(QUERY_PIECE)
     relay(VALUE_PIECE)
     arrive(OUT_PIECE)
-    tally_matrix(3)
+    tally_matrix(3, sta, 0, 3)
     close(KEY_PIECE)
+    relay(LAST_PIECE)
     arrive(QUERY_PIECE)
-    tally_matrix(0)
+    tally_matrix(0, sta, 1, 3)
     close(VALUE_PIECE)
     arrive(KEY_PIECE)
-    tally_matrix(1)
+    tally_matrix(1, sta, 2, 3)
+    spread(1)
+    close(LAST_PIECE)
     take(0)
     for w in range(2):
         mean = gathered_sum(0, 4 * FF + w * LANES, LANES)[:, :1] / D
@@ -1425,13 +1434,18 @@
         ]
         renew(0, 4 + w, mean, tiles, 2 * FF, D * FF)
     arrive(VALUE_PIECE)
-    tally_matrix(2)
+    arrive(LAST_PIECE)
+    tally_matrix(2, r.stv, 0, 1)
     tally_vectors()
+    spread(2)
     take(1)
-    extra = gathered_sum(1, 8 * D, LANES)
-    for j in range(4):
-        renew(1, j, extra[:, j : j + 1] / D, [(j * D, j * D, D)], 4 * D, D * D)
-    size = jnp.sqrt(gathered_sum(1, 8 * D + LANES, LANES) / D)
+    extra = gathered_sum(1, 6 * D, LANES)
+    for at, j in enumerate((3, 0, 1)):
+        renew(1, j, extra[:, at : at + 1] / D, [(at * D, j * D, D)], 3 * D, D * D)
+    take(2)
+    extra = gathered_sum(2, 2 * D, LANES)
+    renew(2, 2, extra[:, :1] / D, [(0, 2 * D, D)], D, D * D)
+    size = jnp.sqrt(gathered_sum(2, 2 * D + LANES, LANES) / D)
     small_new[3] = small[0] - small_new[2] * (vector_rate / jnp.maximum(1.0, size / clip_level))
     scale_new[...] = jnp.where(lane < 6, scale[0], pltpu.roll(size, 6, 1))[:, : scale_new.shape[1]]
     row_all = jnp.zeros((count, LANES), full)
@@ -1452,7 +1466,7 @@
         diagonal(p, p in Z_FIRST).wait_send()
         over_x(p).wait_send()
         over_z(p).wait_send()
-    for n in range(2):
+    for n in range(3):
         for step in range(1, PEERS):
             share(n, step).wait_send()
 
@@ -1525,6 +1539,8 @@
         sta=((1, STAT_A), full),
         srf=((PEERS, 1, STAT_F), full),
         sra=((PEERS, 1, STAT_A), full),
+        stv=((1, STAT_V), full),
+        srv=((PEERS, 1, STAT_V), full),
         small=((3, count, LANES), full),
         small_new=((4, count, LANES), full),
     )
@@ -1538,10 +1554,10 @@
         scratch[f"t_{end}"] = dma((2, 4))
         scratch[f"bt_{end}"] = dma((2, 4))
         scratch[f"core_{end}"] = dma((PIECES + 1,))
-        scratch[f"st_{end}"] = dma((2, PEERS))
+        scratch[f"st_{end}"] = dma((3, PEERS))
     scratch.update(
         own_sem=dma((3,)), keep_sem=dma((2,)), bkeep_sem=dma((2,)), load_sem=dma((20,)),
-        out_sem=dma((PIECES,)), st_keep=dma((2,)),
+        out_sem=dma((PIECES,)), st_keep=dma((3,)),
     )
     return scratch
 

time: 239 us -> 241 us (level)
  no operation moved by 1% of the time
where the time goes in v3:
time: 241 us
  Pallas kernels  240 us (100%)
    pallas_call x1, Pallas kernels, layer(): pl.pallas_call(functools.partial(layer_kernel, LAYER_IN + LAYER_OUT + tup...  230 us
    pallas_call x1, Pallas kernels, finish(): pl.pallas_call(finish_kernel, grid=(TOKENS // SEQ // 2,), out_shape=(jax....  9.41 us

profile of v3, /device:TPU:0, one launch (start us, length us, event | category | flops | bytes accessed | tf_op | source)
XLA Modules:
  0.0 240.6 jit_solution(12996948466032473566)
XLA Ops:
  0.6 230.4 %layer.1 = (bf16[512,768]{1,0:T(8,128)(2,1)}, bf16[512,768]{1,0:T(8,128)(2,1)}, f32[96,9344]{1,0:T(8,128)}, f32[96,128]{1,0:T(8,128)}, f32[1,9216]{1,0:T(1,128)}...) custom-call(f32[4,96,768]{2,1,0:T(8,128)} %bitcast.23, ...), custom_call_target="tpu_custom_call" | custom-call | tf_op jit(solution)/shard_map/layer/pallas_call | solution.py:1582
  231.1 9.4 %finish.1 = (f32[512,768]{1,0:T(8,128)}, f32[512,768]{1,0:T(8,128)}, f32[4,96,768]{2,1,0:T(8,128)}, f32[2,96,3072]{2,1,0:T(8,128)}, f32[4,96,768]{2,1,0:T(8,128)...) custom-call(s32[8]{0:T(128)} %target.1, ...), custom_call_target="tpu_custom_call" | custom-call | tf_op jit(solution)/shard_map/finish/pallas_call | solution.py:1683

commit v4 on v2

--- a/solution.py
+++ b/solution.py
@@ -509,7 +509,7 @@
 OUT_PIECE, QUERY_PIECE, KEY_PIECE, VALUE_PIECE = range(CHUNKS, CHUNKS + 4)
 UP_PIECE = CHUNKS + 4
 PIECES = CHUNKS + 5
-Z_FIRST = (UP_PIECE,)
+Z_FIRST = ()
 RING = 2
 HALF = 384
 SHARD_AT = 2 * LANES

time: 239 us -> 233 us (0.975)
  Pallas kernels: 238 us -> 232 us
    pallas_call x1, Pallas kernels: 228 us -> 223 us  [layer(): pl.pallas_call(functools.partial(layer_kernel, LAYER_IN + LAYER_OUT + tup...]
where the time goes in v4:
time: 233 us
  Pallas kernels  232 us (100%)
    pallas_call x1, Pallas kernels, layer(): pl.pallas_call(functools.partial(layer_kernel, LAYER_IN + LAYER_OUT + tup...  223 us
    pallas_call x1, Pallas kernels, finish(): pl.pallas_call(finish_kernel, grid=(TOKENS // SEQ // 2,), out_shape=(jax....  9.41 us

profile of v4, /device:TPU:0, one launch (start us, length us, event | category | flops | bytes accessed | tf_op | source)
XLA Modules:
  0.0 233.0 jit_solution(13276092778218127816)
XLA Ops:
  0.6 222.7 %layer.1 = (bf16[512,768]{1,0:T(8,128)(2,1)}, bf16[512,768]{1,0:T(8,128)(2,1)}, f32[96,9344]{1,0:T(8,128)}, f32[96,128]{1,0:T(8,128)}, f32[1,9216]{1,0:T(1,128)}...) custom-call(f32[4,96,768]{2,1,0:T(8,128)} %bitcast.23, ...), custom_call_target="tpu_custom_call" | custom-call | tf_op jit(solution)/shard_map/layer/pallas_call | solution.py:1566
  223.4 9.4 %finish.1 = (f32[512,768]{1,0:T(8,128)}, f32[512,768]{1,0:T(8,128)}, f32[4,96,768]{2,1,0:T(8,128)}, f32[2,96,3072]{2,1,0:T(8,128)}, f32[4,96,768]{2,1,0:T(8,128)...) custom-call(s32[8]{0:T(128)} %target.1, ...), custom_call_target="tpu_custom_call" | custom-call | tf_op jit(solution)/shard_map/finish/pallas_call | solution.py:1667
